TPU v7x, 128 devices: a whole 4x4x4 slice. The times are simulated.
128 devices in a mesh: dp: 16 (over z_lo, y, core), inner: 8 (over x, z_hi).
Axes of the slice: x: 4, y: 4, z: 4 (z_hi: 2, z_lo: 2; z = z_hi * 2 + z_lo), core: 2. Of those that a mesh axis runs over, the one named last changes fastest.
Arguments:
- image_embed: bfloat16 [16384, 1152], P(('dp', 'inner')), may hold values from -6 to 6
- text_embed: bfloat16 [16384, 1152], P(('dp', 'inner')), may hold values from -6 to 6
- image_head: bfloat16 [1152, 1152], replicated, may hold values from -0.1875 to 0.1875
- text_head: bfloat16 [1152, 1152], replicated, may hold values from -0.1875 to 0.1875
- pair_ids: int32 [16384], P(('dp', 'inner')), may hold values from 0 to 4095, never falling along the last dimension, each value on 1 to 8 neighbouring positions
- logit_scale: float32 [1], replicated, may hold values from 8 to 24
- logit_bias: float32 [1], replicated, may hold values from -4 to -1.5
Outputs:
- grad_image_head: float32 [1152, 1152], replicated
- grad_text_head: float32 [1152, 1152], replicated
Inputs may be any that keep to these rules, and one draw needn't show every extreme that they name: pair_ids never falls along the pairs; each id covers 1 to 8 consecutive pairs, and some id covers exactly 8.
All inputs are finite; a program needn't handle non-finite values.
Results may differ from a plain program's by a relative error of at most 0.0025.
Values may be sent and summed in bfloat16 or wider, within the bound.
No kernel may reach another device: no remote copies, remote signals or barrier semaphores. Data moves between devices by JAX's collectives and lax.ppermute only.
A program may use at most 128 MiB of HBM per device.

v0:
```python
import functools
import math

import jax
import jax.numpy as jnp
from jax import lax
from jax.experimental import pallas as pl
from jax.experimental.pallas import tpu as pltpu
from jax.sharding import Mesh, PartitionSpec as P

AXES = ("zl", "y", "c", "x", "zh")
SIZES = (2, 4, 2, 4, 2)
BF16 = jnp.bfloat16
F32 = jnp.float32
WIDE = 1152
ROWS = 2048
VMEM_BYTES = 48 * 1024 * 1024


def routes(move):
    pairs = []
    index = 0
    for zl in range(2):
        for y in range(4):
            for c in range(2):
                for x in range(4):
                    for zh in range(2):
                        tzl, ty, tc, tx, tzh = move(zl, y, c, x, zh)
                        pairs.append((index, (((tzl * 4 + ty) * 2 + tc) * 4 + tx) * 2 + tzh))
                        index += 1
    return pairs


def send(value, move):
    return lax.ppermute(value, AXES, routes(move))


def other_core(zl, y, c, x, zh):
    return (zl, y, 1 - c, x, zh)


def z_pair(swap):
    def move(zl, y, c, x, zh):
        return (1 - zl, y, c, x, zh if (c ^ swap) == 0 else 1 - zh)

    return move


def ring(by, swap):
    def move(zl, y, c, x, zh):
        if (c ^ swap) == 0:
            return (zl, y, c, (x + by) % 4, zh)
        return (zl, (y + by) % 4, c, x, zh)

    return move


def z_ring(by):
    def move(zl, y, c, x, zh):
        z = (zh * 2 + zl + by) % 4
        return (z % 2, y, c, x, z // 2)

    return move


def eye_256():
    return lax.broadcasted_iota(jnp.int32, (256, 256), 0) == lax.broadcasted_iota(
        jnp.int32, (256, 256), 1
    )


def as_column(row):
    return jnp.sum(jnp.where(eye_256(), row, 0.0), axis=1, keepdims=True)


def id_row(coded):
    coded = coded.astype(F32)
    parts = [coded[i : i + 1, :128] * 64.0 + coded[i : i + 1, 128:256] for i in (0, 16)]
    return jnp.concatenate(parts, axis=1)


def project_kernel(near, far, head_near, head_far, message, rows_near):
    sides = ((near, head_near, rows_near, 0, 0), (far, head_far, message, 576, 288))
    for block, head, rows, at, to in sides:
        rows[at : at + 256, :] = block[:256, :]
        projected = jnp.dot(block[:256, :], head[...], preferred_element_type=F32)
        inverse = lax.rsqrt(jnp.sum(projected * projected, axis=1, keepdims=True) + 1e-06)
        message[to : to + 256, :] = (projected * inverse).astype(BF16)
        message[to + 256 : to + 288, :] = block[256:288, :]
        rest = jnp.sum(jnp.where(eye_256(), inverse, 0.0), axis=0, keepdims=True)
        lines = lax.broadcasted_iota(jnp.int32, (16, 256), 0)
        coded = block[256:272, :256].astype(F32)
        for line in (1, 2, 3):
            part = rest.astype(BF16).astype(F32)
            coded = jnp.where(lines == line, part, coded)
            rest = rest - part
        message[to + 256 : to + 272, :256] = coded.astype(BF16)


def project(near, far, heads):
    whole = pl.BlockSpec(memory_space=pltpu.VMEM)
    return pl.pallas_call(
        project_kernel,
        out_shape=[
            jax.ShapeDtypeStruct((832, WIDE), BF16),
            jax.ShapeDtypeStruct((256, WIDE), BF16),
        ],
        in_specs=[whole] * 4,
        out_specs=[whole] * 2,
        compiler_params=pltpu.CompilerParams(vmem_limit_bytes=28 * 1024 * 1024),
        cost_estimate=pl.CostEstimate(
            flops=2 * 512 * WIDE * WIDE, bytes_accessed=8_000_000, transcendentals=0
        ),
        name="project",
    )(near, far, *heads)


def unit_loads(sources, units, ids, unit_sems, id_sems):
    loads = []
    for i, (source, start) in enumerate(sources):
        rows = source.at[pl.ds(start, 256), :]
        coded = source.at[pl.ds(start + 256, 32), pl.ds(0, 256)]
        loads.append(
            (
                pltpu.make_async_copy(rows, units.at[pl.ds(i * 256, 256), :], unit_sems.at[i]),
                pltpu.make_async_copy(coded, ids.at[i], id_sems.at[i]),
            )
        )
    return loads


def pair_coefs(knob_ref, near, column, unit, ids, coef, parts):
    half_scale, half_bias, half = knob_ref[0], knob_ref[1], knob_ref[2]
    for part in parts:
        cosine = lax.dot_general(
            near,
            unit[part * 256 : part * 256 + 256, :],
            (((1,), (1,)), ((), ())),
            preferred_element_type=F32,
        )
        base = jnp.where(column == id_row(ids[part]), -half, half)
        value = jnp.tanh(cosine * half_scale + half_bias) * half + base
        coef[:, pl.ds(part * 256, 256)] = value.astype(BF16)


def chunk_column(ids, step):
    return jnp.concatenate([as_column(id_row(ids[2 * step + i])) for i in range(2)], axis=0)


def chunk_inverse(ids, step):
    parts = []
    for i in range(2):
        coded = ids[2 * step + i].astype(F32)
        parts.append(as_column(coded[1:2] + coded[2:3] + coded[3:4]))
    return jnp.concatenate(parts, axis=0)


def unit_sources(own, over):
    near, far = [], []
    for mine, theirs in zip(own, over):
        near += [(mine, 0), (theirs, 288)]
        far += [(mine, 288), (theirs, 0)]
    return near, far


def early_kernel(knob_ref, *refs):
    near_sources, far_sources = unit_sources(refs[:3], refs[3:6])
    grad, near, near_ids, far, far_ids, coef, sems = refs[6:]
    step = pl.program_id(0)
    near_loads = unit_loads(near_sources, near, near_ids, sems.at[0], sems.at[1])
    far_loads = unit_loads(far_sources, far, far_ids, sems.at[2], sems.at[3])

    @pl.when(step == 0)
    def _():
        for pair in far_loads + near_loads:
            for load in pair:
                load.start()
        for pair in far_loads:
            for load in pair:
                load.wait()

    for i, pair in enumerate(near_loads):

        @pl.when(step == i // 2)
        def _(pair=pair):
            for load in pair:
                load.wait()

    rows = near[pl.ds(pl.multiple_of(step * 512, 512), 512), :]
    pair_coefs(knob_ref, rows, chunk_column(near_ids, step), far, far_ids, coef, range(6))
    grad[...] = jnp.dot(coef[...], far[...], preferred_element_type=F32)


def early_pairs(knobs, own, over):
    return pl.pallas_call(
        early_kernel,
        grid=(3,),
        out_shape=jax.ShapeDtypeStruct((1536, WIDE), F32),
        in_specs=[pl.BlockSpec(memory_space=pltpu.SMEM)]
        + [pl.BlockSpec(memory_space=pl.ANY)] * 6,
        out_specs=pl.BlockSpec((512, WIDE), lambda i: (i, 0)),
        scratch_shapes=[
            pltpu.VMEM((1536, WIDE), BF16),
            pltpu.VMEM((6, 32, 256), BF16),
            pltpu.VMEM((1536, WIDE), BF16),
            pltpu.VMEM((6, 32, 256), BF16),
            pltpu.VMEM((512, 1536), BF16),
            pltpu.SemaphoreType.DMA((4, 6)),
        ],
        compiler_params=pltpu.CompilerParams(
            dimension_semantics=("arbitrary",), vmem_limit_bytes=40 * 1024 * 1024
        ),
        cost_estimate=pl.CostEstimate(
            flops=4 * 1536 * 1536 * WIDE, bytes_accessed=14_000_000, transcendentals=1536 * 1536
        ),
        name="early_pairs",
    )(knobs, *own, *over)


def late_kernel(at_ref, knob_ref, early, *refs):
    own, over, own_rows, outs = refs[:4], refs[4:8], refs[8:12], refs[12:16]
    near, near_ids, far, far_ids, rows, grad, coef, total, sems, more_sems = refs[16:]
    near_sources, far_sources = unit_sources(own, over)
    step = pl.program_id(0)
    near_loads = unit_loads(near_sources, near, near_ids, sems.at[0], sems.at[1])
    far_loads = unit_loads(far_sources, far, far_ids, sems.at[2], sems.at[3])
    for i in range(8):
        source = over[i // 2].at[pl.ds(576, 256), :] if i % 2 else own_rows[i // 2]
        near_loads[i] += (
            pltpu.make_async_copy(source, rows.at[pl.ds(i * 256, 256), :], more_sems.at[0, i]),
        )
    for i in range(3):
        near_loads[2 * i] += (
            pltpu.make_async_copy(
                early.at[pl.ds(512 * i, 512), :], grad.at[i], more_sems.at[1, i]
            ),
        )

    @pl.when(step == 0)
    def _():
        for pair in far_loads[6:] + near_loads[:2]:
            for load in pair:
                load.start()
        for pair in far_loads[6:]:
            for load in pair:
                load.wait()
        total[...] = jnp.zeros_like(total)

    for i, pair in enumerate(near_loads):

        @pl.when(step == i // 2)
        def _(pair=pair):
            for load in pair:
                load.wait()

    @pl.when(step == 0)
    def _():
        for pair in near_loads[2:] + far_loads[:6]:
            for load in pair:
                load.start()

    at = pl.ds(pl.multiple_of(step * 512, 512), 512)
    column = chunk_column(near_ids, step)
    inverse = chunk_inverse(near_ids, step)

    def finish(gradient):
        direction = near[at, :].astype(F32)
        radial = jnp.sum(gradient * direction, axis=1, keepdims=True)
        back = ((gradient - radial * direction) * inverse).astype(BF16)
        total[...] += lax.dot_general(
            rows[at, :], back, (((0,), (0,)), ((), ())), preferred_element_type=F32
        )

    @pl.when(step < 3)
    def _():
        pair_coefs(knob_ref, near[at, :], column, far, far_ids, coef, (6, 7))
        more = jnp.dot(coef[:, 1536:], far[1536:, :], preferred_element_type=F32)
        finish(grad[step] + more)

    @pl.when(step == 3)
    def _():
        for pair in far_loads[:6]:
            for load in pair:
                load.wait()
        pair_coefs(knob_ref, near[at, :], column, far, far_ids, coef, range(8))
        finish(jnp.dot(coef[...], far[...], preferred_element_type=F32))
        for by, out in zip((0, 1, 3, 2), outs):
            place = pl.multiple_of(lax.rem(at_ref[0] + by, 4) * 288, 288)
            out[...] = total[pl.ds(place, 288), :].astype(out.dtype)


def late_pairs(at, knobs, early, own, over, own_rows):
    smem = pl.BlockSpec(memory_space=pltpu.SMEM)
    return pl.pallas_call(
        late_kernel,
        grid=(4,),
        out_shape=[jax.ShapeDtypeStruct((288, WIDE), kind) for kind in (F32, BF16, BF16, BF16)],
        in_specs=[smem, smem] + [pl.BlockSpec(memory_space=pl.ANY)] * 13,
        out_specs=[
            pl.BlockSpec((288, WIDE), lambda i: (0, 0), pipeline_mode=pl.Buffered(1))
        ]
        * 4,
        scratch_shapes=[
            pltpu.VMEM((ROWS, WIDE), BF16),
            pltpu.VMEM((8, 32, 256), BF16),
            pltpu.VMEM((ROWS, WIDE), BF16),
            pltpu.VMEM((8, 32, 256), BF16),
            pltpu.VMEM((ROWS, WIDE), BF16),
            pltpu.VMEM((3, 512, WIDE), F32),
            pltpu.VMEM((512, ROWS), BF16),
            pltpu.VMEM((WIDE, WIDE), F32),
            pltpu.SemaphoreType.DMA((4, 8)),
            pltpu.SemaphoreType.DMA((2, 8)),
        ],
        compiler_params=pltpu.CompilerParams(
            dimension_semantics=("arbitrary",), vmem_limit_bytes=VMEM_BYTES
        ),
        cost_estimate=pl.CostEstimate(
            flops=4 * 7 * 512 * 512 * WIDE + 2 * ROWS * WIDE * WIDE,
            bytes_accessed=25_000_000,
            transcendentals=7 * 512 * 512,
        ),
        name="late_pairs",
    )(at, knobs, early, *own, *over, *own_rows)


def place_kernel(heads, where_ref, *refs):
    count = len(heads)
    pieces, outs = refs[:count], refs[-6:-4]
    narrow, wide, in_sems, out_sems = refs[-4:]
    loads = [
        pltpu.make_async_copy(piece, narrow.at[i], in_sems.at[i]) for i, piece in enumerate(pieces)
    ]
    for load in loads:
        load.start()

    def stores(i):
        head = where_ref[0] if heads[i] == 0 else 1 - where_ref[0]
        row = pl.multiple_of(where_ref[1 + i] * 288, 288)
        for h in range(2):
            copy = pltpu.make_async_copy(
                wide.at[i], outs[h].at[pl.ds(row, 288), :], out_sems.at[i]
            )
            yield head == h, copy

    for i in range(count):
        loads[i].wait()
        wide[i] = narrow[i].astype(F32)
        for here, copy in stores(i):
            pl.when(here)(copy.start)
    for i in range(count):
        for here, copy in stores(i):
            pl.when(here)(copy.wait)


def place(where, heads, pieces, held):
    count = len(pieces)
    hbm = pl.BlockSpec(memory_space=pl.ANY)
    return pl.pallas_call(
        functools.partial(place_kernel, heads),
        out_shape=[jax.ShapeDtypeStruct((WIDE, WIDE), F32)] * 2,
        in_specs=[pl.BlockSpec(memory_space=pltpu.SMEM)] + [hbm] * (count + len(held)),
        out_specs=[hbm] * 2,
        input_output_aliases={1 + count + i: i for i in range(len(held))},
        scratch_shapes=[
            pltpu.VMEM((count, 288, WIDE), BF16),
            pltpu.VMEM((count, 288, WIDE), F32),
            pltpu.SemaphoreType.DMA((count,)),
            pltpu.SemaphoreType.DMA((count,)),
        ],
        compiler_params=pltpu.CompilerParams(vmem_limit_bytes=32 * 1024 * 1024),
        name="place",
    )(where, *pieces, *held)


def added(total, parts):
    for part in parts:
        total = total + part.astype(F32)
    return total


def scattered(value, by_route, mine):
    rows = value.shape[0] // 4
    total = lax.dynamic_slice_in_dim(value, mine * rows, rows, 0)
    parts = []
    for by in (1, 3, 2):
        part = lax.dynamic_slice_in_dim(value, lax.rem(mine + by, 4) * rows, rows, 0)
        parts.append(send(part, by_route(by)))
    return added(total, parts)


def local(image_embed, text_embed, image_head, text_head, pair_ids, logit_scale, logit_bias):
    first = lax.axis_index("c") == 0
    scale = logit_scale[0]
    half = scale * (0.5 / math.sqrt(16384))
    knobs = jnp.stack([scale * 0.5, logit_bias[0] * 0.5, half])

    ids_row = jnp.concatenate(
        [(pair_ids // 64).astype(BF16), (pair_ids % 64).astype(BF16), jnp.zeros((896,), BF16)]
    )[None]
    ids_rows = jnp.concatenate([ids_row, jnp.zeros((15, WIDE), BF16)], axis=0)
    mine = jnp.concatenate([jnp.where(first, image_embed, text_embed), ids_rows], axis=0)
    theirs = jnp.concatenate([jnp.where(first, text_embed, image_embed), ids_rows], axis=0)
    heads = (jnp.where(first, image_head, text_head), jnp.where(first, text_head, image_head))

    got = [send(mine, z_pair(0)), send(theirs, z_pair(1))]
    mine, theirs = [
        jnp.concatenate([block[:128], other[:128], block[128:], other[128:]], axis=0)
        for block, other in zip((mine, theirs), got)
    ]
    blocks = [(mine, theirs)]
    for by in (1, 3, 2):
        blocks.append((send(mine, ring(by, 0)), send(theirs, ring(by, 1))))
    own, over, own_rows = [], [], []

    def take(turn):
        message, rows = project(*blocks[turn], heads)
        own.append(message)
        over.append(send(message, other_core))
        own_rows.append(rows)

    for turn in range(3):
        take(turn)
    early = early_pairs(knobs, own, over)
    blocks[3], early = lax.optimization_barrier((blocks[3], early))
    take(3)

    at_x = lax.axis_index("x")
    at_y = lax.axis_index("y")
    at_first = jnp.where(first, at_x, at_y)
    at_second = jnp.where(first, at_y, at_x)
    part, *away = late_pairs(at_first[None], knobs, early, own, over, own_rows)
    part = added(part, [send(piece, ring(by, 0)) for by, piece in zip((1, 3, 2), away)])
    part = scattered(part, lambda by: ring(by, 1), at_second)
    moved = [send(part, z_ring(by)) for by in (1, 3, 2)]
    at_z = lax.axis_index("zh") * 2 + lax.axis_index("zl")
    stack = jnp.zeros((4,) + part.shape, F32)
    for by, piece in zip((0, 1, 3, 2), [part] + moved):
        stack = lax.dynamic_update_slice_in_dim(stack, piece[None], lax.rem(at_z + 4 - by, 4), 0)
    part = ((stack[0] + stack[1]) + (stack[2] + stack[3])).astype(BF16)

    quarter = jnp.zeros((288, WIDE), BF16)
    for by in (0, 1, 3, 2):
        piece = part if by == 0 else send(part, ring(by, 1))
        quarter = lax.dynamic_update_slice_in_dim(
            quarter, piece, lax.rem(at_second + 4 - by, 4) * 72, 0
        )
    core = lax.axis_index("c")

    def where(bys):
        places = [lax.rem(at + 4 - by, 4) for at in (at_first, at_second) for by in bys]
        return jnp.stack([core] + places).astype(jnp.int32)

    pieces = [quarter] + [send(quarter, ring(by, 0)) for by in (1, 3, 2)]
    pieces = pieces + [send(piece, other_core) for piece in pieces]
    places = [lax.rem(at + 4 - by, 4) for at in (at_first, at_second) for by in (0, 1, 3, 2)]
    where = jnp.stack([lax.axis_index("c")] + places).astype(jnp.int32)
    return tuple(place(where, (0, 0, 0, 0, 1, 1, 1, 1), pieces, ()))


def solution(mesh):
    split = Mesh(mesh.devices.reshape(SIZES), AXES)
    every = P(AXES)
    return jax.shard_map(
        local,
        mesh=split,
        in_specs=(every, every, P(), P(), every, P(), P()),
        out_specs=(P(), P()),
        check_vma=False,
    )
```

profile of v0, /device:TPU:1, one launch (start us, length us, event | category | flops | bytes accessed | tf_op | source)
XLA Modules:
  0.0 194.3 jit_solution(15021280858302054739)
XLA Ops:
  2.5 2.5 %collective-permute-start.2 = (bf16[144,1152]{1,0:T(8,128)(2,1)S(1)}, bf16[144,1152]{1,0:T(8,128)(2,1)S(1)}, u32[]{:S(2)}, u32[]{:S(2)}) collective-permute-start(bf16[144,1152]{1,0:T(8,128)(2,1)S(1)} %get-tuple-element.43), channel_id=1, source_target_pairs={{0,65},{1,64},{2,67},{3,66},{4,69},{5,68},{6,71},{7,70},{8,72},{9,... | collective-permute-start | bytes 995336 | tf_op jit(solution)/shard_map/ppermute | solution.py:35
  7.3 2.6 %collective-permute-done.2 = bf16[144,1152]{1,0:T(8,128)(2,1)S(1)} collective-permute-done((bf16[144,1152]{1,0:T(8,128)(2,1)S(1)}, bf16[144,1152]{1,0:T(8,128)(2,1)S(1)}, u32[]{:S(2)}, u32[]{:S(2)}) %collective-permute-start.2) | collective-permute-done | bytes 331808 | tf_op jit(solution)/shard_map/ppermute | solution.py:35
  10.4 2.5 %collective-permute-start.7 = (bf16[288,1152]{1,0:T(8,128)(2,1)S(1)}, bf16[288,1152]{1,0:T(8,128)(2,1)S(1)}, u32[]{:S(2)}, u32[]{:S(2)}) collective-permute-start(bf16[288,1152]{1,0:T(8,128)(2,1)S(1)} %concatenate.24.far), channel_id=1, source_target_pairs={{0,48},{1,49},{2,50},{3,51},{4,52},{5,53},{6,54},{7,55},{8,14},{9,... | collective-permute-start | bytes 1990664 | tf_op jit(solution)/shard_map/ppermute | solution.py:35
  13.0 2.8 %collective-permute-done = bf16[144,1152]{1,0:T(8,128)(2,1)S(1)} collective-permute-done((bf16[144,1152]{1,0:T(8,128)(2,1)S(1)}, bf16[144,1152]{1,0:T(8,128)(2,1)S(1)}, u32[]{:S(2)}, u32[]{:S(2)}) %collective-permute-start) | collective-permute-done | bytes 331808 | tf_op jit(solution)/shard_map/ppermute | solution.py:35
  16.3 2.8 %collective-permute-start.6 = (bf16[288,1152]{1,0:T(8,128)(2,1)S(1)}, bf16[288,1152]{1,0:T(8,128)(2,1)S(1)}, u32[]{:S(2)}, u32[]{:S(2)}) collective-permute-start(bf16[288,1152]{1,0:T(8,128)(2,1)S(1)} %concatenate.22.near), channel_id=1, source_target_pairs={{0,6},{1,7},{2,0},{3,1},{4,2},{5,3},{6,4},{7,5},{8,56},{9,57},{10,... | collective-permute-start | bytes 1990664 | tf_op jit(solution)/shard_map/ppermute | solution.py:35
  19.1 3.0 %broadcast_select_fusion = (bf16[1152,1152]{1,0:T(8,128)(2,1)S(1)}, bf16[1152,1152]{1,0:T(8,128)(2,1)S(1)}) fusion(bf16[1152,1152]{1,0:T(8,128)(2,1)} %param.10, bf16[1152,1152]{1,0:T(8,128)(2,1)} %param.9, pred[]{:T(512)S(6)} %eq.5), kind=kLoop, calls=%fused_computation | loop fusion | flops 2654208 | bytes 10616833 | tf_op jit(solution)/shard_map/jit(_where)/select_n | solution.py:404
  24.3 4.4 %collective-permute-start.8 = (bf16[832,1152]{1,0:T(8,128)(2,1)S(1)}, bf16[832,1152]{1,0:T(8,128)(2,1)S(1)}, u32[]{:S(2)}, u32[]{:S(2)}) collective-permute-start(bf16[832,1152]{1,0:T(8,128)(2,1)S(1)} %get-tuple-element.17.refs_0_), channel_id=1, source_target_pairs={{0,8},{1,9},{2,10},{3,11},{4,12},{5,13},{6,14},{7,15},{8,0},{9,1},... | collective-permute-start | bytes 5750792 | tf_op jit(solution)/shard_map/ppermute | solution.py:35
  28.7 4.0 %collective-permute-done.6.near = bf16[288,1152]{1,0:T(8,128)(2,1)S(1)} collective-permute-done((bf16[288,1152]{1,0:T(8,128)(2,1)S(1)}, bf16[288,1152]{1,0:T(8,128)(2,1)S(1)}, u32[]{:S(2)}, u32[]{:S(2)}) %collective-permute-start.6) | collective-permute-done | bytes 663584 | tf_op jit(solution)/shard_map/ppermute | solution.py:35
  41.2 2.8 %collective-permute-start.3 = (bf16[288,1152]{1,0:T(8,128)(2,1)S(1)}, bf16[288,1152]{1,0:T(8,128)(2,1)S(1)}, u32[]{:S(2)}, u32[]{:S(2)}) collective-permute-start(bf16[288,1152]{1,0:T(8,128)(2,1)S(1)} %concatenate.24.far), channel_id=1, source_target_pairs={{0,32},{1,33},{2,34},{3,35},{4,36},{5,37},{6,38},{7,39},{8,12},{9,... | collective-permute-start | bytes 1990664 | tf_op jit(solution)/shard_map/ppermute | solution.py:35
  45.4 17.1 %early_pairs.1.early = f32[1536,1152]{1,0:T(8,128)} custom-call(f32[3]{0:T(128)S(1)} %pad_maximum_fusion.5.knob_ref, bf16[832,1152]{1,0:T(8,128)(2,1)S(1)} %get-tuple-element.17.refs_0_, bf16[832,1152]{1,0:T(8,128)(2,1)S(1)} %get-tuple-element.18.refs_1_, bf16[832,1152]{1,0:T(8,128)(2,1)S(1)} %get-tuple-element.19.refs_2_, ...), custom_call_target="tpu_custom_call" | custom-call | flops 10871635968 | bytes 14000000 | tf_op jit(solution)/shard_map/early_pairs/pallas_call | solution.py:195
  66.5 3.7 %collective-permute-done.11.refs_7_ = bf16[832,1152]{1,0:T(8,128)(2,1)} collective-permute-done((bf16[832,1152]{1,0:T(8,128)(2,1)S(1)}, bf16[832,1152]{1,0:T(8,128)(2,1)}, u32[]{:S(2)}, u32[]{:S(2)}) %collective-permute-start.11) | collective-permute-done | bytes 1916960 | tf_op jit(solution)/shard_map/ppermute | solution.py:35
  74.4 26.4 %late_pairs.1 = (f32[288,1152]{1,0:T(8,128)S(1)}, bf16[288,1152]{1,0:T(8,128)(2,1)}, bf16[288,1152]{1,0:T(8,128)(2,1)}, bf16[288,1152]{1,0:T(8,128)(2,1)}) custom-call(s32[1]{0:T(128)} %bitcast.9.at_ref, f32[3]{0:T(128)S(1)} %pad_maximum_fusion.5.knob_ref, f32[1536,1152]{1,0:T(8,128)} %early_pairs.1.early, bf16[832,1152]{1,0:T(8,128)(2,1)} %copy-done, ...), custom_call_target="tpu_custom_call" | custom-call | flops 13891534848 | bytes 25000000 | tf_op jit(solution)/shard_map/late_pairs/pallas_call | solution.py:294
  104.3 14.9 %collective-permute-done.12 = bf16[288,1152]{1,0:T(8,128)(2,1)S(1)} collective-permute-done((bf16[288,1152]{1,0:T(8,128)(2,1)}, bf16[288,1152]{1,0:T(8,128)(2,1)S(1)}, u32[]{:S(2)}, u32[]{:S(2)}) %collective-permute-start.12) | collective-permute-done | bytes 663584 | tf_op jit(solution)/shard_map/ppermute | solution.py:35
  125.3 8.5 %collective-permute-done.15 = f32[72,1152]{1,0:T(8,128)S(1)} collective-permute-done((f32[72,1152]{1,0:T(8,128)S(1)}, f32[72,1152]{1,0:T(8,128)S(1)}, u32[]{:S(2)}, u32[]{:S(2)}) %collective-permute-start.15) | collective-permute-done | bytes 331808 | tf_op jit(solution)/shard_map/ppermute | solution.py:35
  135.8 2.6 %collective-permute-start.19 = (f32[72,1152]{1,0:T(8,128)S(1)}, f32[72,1152]{1,0:T(8,128)S(1)}, u32[]{:S(2)}, u32[]{:S(2)}) collective-permute-start(f32[72,1152]{1,0:T(8,128)S(1)} %get-tuple-element.35), channel_id=1, source_target_pairs={{0,65},{1,64},{2,67},{3,66},{4,69},{5,68},{6,71},{7,70},{8,73},{9,... | collective-permute-start | bytes 995336 | tf_op jit(solution)/shard_map/ppermute | solution.py:35
  139.3 6.5 %collective-permute-done.18 = f32[72,1152]{1,0:T(8,128)S(1)} collective-permute-done((f32[72,1152]{1,0:T(8,128)S(1)}, f32[72,1152]{1,0:T(8,128)S(1)}, u32[]{:S(2)}, u32[]{:S(2)}) %collective-permute-start.18) | collective-permute-done | bytes 331808 | tf_op jit(solution)/shard_map/ppermute | solution.py:35
  145.9 5.4 %collective-permute-done.20 = f32[72,1152]{1,0:T(8,128)S(1)} collective-permute-done((f32[72,1152]{1,0:T(8,128)S(1)}, f32[72,1152]{1,0:T(8,128)S(1)}, u32[]{:S(2)}, u32[]{:S(2)}) %collective-permute-start.20) | collective-permute-done | bytes 331808 | tf_op jit(solution)/shard_map/ppermute | solution.py:35
  152.0 3.6 %collective-permute-start.22 = (bf16[72,1152]{1,0:T(8,128)(2,1)S(1)}, bf16[72,1152]{1,0:T(8,128)(2,1)S(1)}, u32[]{:S(2)}, u32[]{:S(2)}) collective-permute-start(bf16[72,1152]{1,0:T(8,128)(2,1)S(1)} %get-tuple-element.33), channel_id=1, source_target_pairs={{0,48},{1,49},{2,50},{3,51},{4,52},{5,53},{6,54},{7,55},{8,14},{9,... | collective-permute-start | bytes 497672 | tf_op jit(solution)/shard_map/ppermute | solution.py:35
  158.4 3.0 %collective-permute-done.23 = bf16[72,1152]{1,0:T(8,128)(2,1)S(1)} collective-permute-done((bf16[72,1152]{1,0:T(8,128)(2,1)S(1)}, bf16[72,1152]{1,0:T(8,128)(2,1)S(1)}, u32[]{:S(2)}, u32[]{:S(2)}) %collective-permute-start.23) | collective-permute-done | bytes 165920 | tf_op jit(solution)/shard_map/ppermute | solution.py:35
  161.5 2.7 %collective-permute-start.25 = (bf16[288,1152]{1,0:T(8,128)(2,1)S(1)}, bf16[288,1152]{1,0:T(8,128)(2,1)S(1)}, u32[]{:S(2)}, u32[]{:S(2)}) collective-permute-start(bf16[288,1152]{1,0:T(8,128)(2,1)S(1)} %constant_dynamic-update-slice_fusion.refs_0_), channel_id=1, source_target_pairs={{0,6},{1,7},{2,0},{3,1},{4,2},{5,3},{6,4},{7,5},{8,56},{9,57},{10,... | collective-permute-start | bytes 1990664 | tf_op jit(solution)/shard_map/ppermute | solution.py:35
  164.1 6.5 %collective-permute-start.27 = (bf16[288,1152]{1,0:T(8,128)(2,1)S(1)}, bf16[288,1152]{1,0:T(8,128)(2,1)S(1)}, u32[]{:S(2)}, u32[]{:S(2)}) collective-permute-start(bf16[288,1152]{1,0:T(8,128)(2,1)S(1)} %constant_dynamic-update-slice_fusion.refs_0_), channel_id=1, source_target_pairs={{0,8},{1,9},{2,10},{3,11},{4,12},{5,13},{6,14},{7,15},{8,0},{9,1},... | collective-permute-start | bytes 1990664 | tf_op jit(solution)/shard_map/ppermute | solution.py:35
  170.6 9.0 %collective-permute-done.24.refs_1_ = bf16[288,1152]{1,0:T(8,128)(2,1)S(1)} collective-permute-done((bf16[288,1152]{1,0:T(8,128)(2,1)S(1)}, bf16[288,1152]{1,0:T(8,128)(2,1)S(1)}, u32[]{:S(2)}, u32[]{:S(2)}) %collective-permute-start.24) | collective-permute-done | bytes 663584 | tf_op jit(solution)/shard_map/ppermute | solution.py:35
  179.6 5.0 %collective-permute-start.29 = (bf16[288,1152]{1,0:T(8,128)(2,1)S(1)}, bf16[288,1152]{1,0:T(8,128)(2,1)}, u32[]{:S(2)}, u32[]{:S(2)}) collective-permute-start(bf16[288,1152]{1,0:T(8,128)(2,1)S(1)} %collective-permute-done.25.refs_2_), channel_id=1, source_target_pairs={{0,8},{1,9},{2,10},{3,11},{4,12},{5,13},{6,14},{7,15},{8,0},{9,1},... | collective-permute-start | bytes 1990664 | tf_op jit(solution)/shard_map/ppermute | solution.py:35
  188.2 5.8 %place.1 = (f32[1152,1152]{1,0:T(8,128)}, f32[1152,1152]{1,0:T(8,128)}) custom-call(s32[9]{0:T(128)S(1)} %stack.45.where_ref, bf16[288,1152]{1,0:T(8,128)(2,1)S(1)} %constant_dynamic-update-slice_fusion.refs_0_, bf16[288,1152]{1,0:T(8,128)(2,1)S(1)} %collective-permute-done.24.refs_1_, bf16[288,1152]{1,0:T(8,128)(2,1)S(1)} %collective-permute-done.25.refs_2_, ...), custom_call_target="tpu_custom_call" | custom-call | tf_op jit(solution)/shard_map/place/pallas_call | solution.py:359
  (109 shorter events, 43.7 us)
Async XLA Ops:
  2.5 7.3 %collective-permute-start.2 = (bf16[144,1152]{1,0:T(8,128)(2,1)S(1)}, bf16[144,1152]{1,0:T(8,128)(2,1)S(1)}, u32[]{:S(2)}, u32[]{:S(2)}) collective-permute-start(bf16[144,1152]{1,0:T(8,128)(2,1)S(1)} %get-tuple-element.43), channel_id=1, source_target_pairs={{0,65},{1,64},{2,67},{3,66},{4,69},{5,68},{6,71},{7,70},{8,72},{9,... | collective-permute-start | bytes 995336 | tf_op jit(solution)/shard_map/ppermute | solution.py:35
  5.1 10.7 %collective-permute-start = (bf16[144,1152]{1,0:T(8,128)(2,1)S(1)}, bf16[144,1152]{1,0:T(8,128)(2,1)S(1)}, u32[]{:S(2)}, u32[]{:S(2)}) collective-permute-start(bf16[144,1152]{1,0:T(8,128)(2,1)S(1)} %get-tuple-element.44), channel_id=1, source_target_pairs={{0,64},{1,65},{2,66},{3,67},{4,68},{5,69},{6,70},{7,71},{8,73},{9,... | collective-permute-start | bytes 995336 | tf_op jit(solution)/shard_map/ppermute | solution.py:35
  10.4 18.3 %collective-permute-start.7 = (bf16[288,1152]{1,0:T(8,128)(2,1)S(1)}, bf16[288,1152]{1,0:T(8,128)(2,1)S(1)}, u32[]{:S(2)}, u32[]{:S(2)}) collective-permute-start(bf16[288,1152]{1,0:T(8,128)(2,1)S(1)} %concatenate.24.far), channel_id=1, source_target_pairs={{0,48},{1,49},{2,50},{3,51},{4,52},{5,53},{6,54},{7,55},{8,14},{9,... | collective-permute-start | bytes 1990664 | tf_op jit(solution)/shard_map/ppermute | solution.py:35
  13.0 23.5 %collective-permute-start.5 = (bf16[288,1152]{1,0:T(8,128)(2,1)S(1)}, bf16[288,1152]{1,0:T(8,128)(2,1)S(1)}, u32[]{:S(2)}, u32[]{:S(2)}) collective-permute-start(bf16[288,1152]{1,0:T(8,128)(2,1)S(1)} %concatenate.24.far), channel_id=1, source_target_pairs={{0,16},{1,17},{2,18},{3,19},{4,20},{5,21},{6,22},{7,23},{8,10},{9,... | collective-permute-start | bytes 1990664 | tf_op jit(solution)/shard_map/ppermute | solution.py:35
  16.3 16.3 %collective-permute-start.6 = (bf16[288,1152]{1,0:T(8,128)(2,1)S(1)}, bf16[288,1152]{1,0:T(8,128)(2,1)S(1)}, u32[]{:S(2)}, u32[]{:S(2)}) collective-permute-start(bf16[288,1152]{1,0:T(8,128)(2,1)S(1)} %concatenate.22.near), channel_id=1, source_target_pairs={{0,6},{1,7},{2,0},{3,1},{4,2},{5,3},{6,4},{7,5},{8,56},{9,57},{10,... | collective-permute-start | bytes 1990664 | tf_op jit(solution)/shard_map/ppermute | solution.py:35
  19.1 17.4 %collective-permute-start.4 = (bf16[288,1152]{1,0:T(8,128)(2,1)S(1)}, bf16[288,1152]{1,0:T(8,128)(2,1)S(1)}, u32[]{:S(2)}, u32[]{:S(2)}) collective-permute-start(bf16[288,1152]{1,0:T(8,128)(2,1)S(1)} %concatenate.22.near), channel_id=1, source_target_pairs={{0,2},{1,3},{2,4},{3,5},{4,6},{5,7},{6,0},{7,1},{8,24},{9,25},{10,... | collective-permute-start | bytes 1990664 | tf_op jit(solution)/shard_map/ppermute | solution.py:35
  24.3 21.0 %collective-permute-start.8 = (bf16[832,1152]{1,0:T(8,128)(2,1)S(1)}, bf16[832,1152]{1,0:T(8,128)(2,1)S(1)}, u32[]{:S(2)}, u32[]{:S(2)}) collective-permute-start(bf16[832,1152]{1,0:T(8,128)(2,1)S(1)} %get-tuple-element.17.refs_0_), channel_id=1, source_target_pairs={{0,8},{1,9},{2,10},{3,11},{4,12},{5,13},{6,14},{7,15},{8,0},{9,1},... | collective-permute-start | bytes 5750792 | tf_op jit(solution)/shard_map/ppermute | solution.py:35
  34.8 10.5 %collective-permute-start.10 = (bf16[832,1152]{1,0:T(8,128)(2,1)S(1)}, bf16[832,1152]{1,0:T(8,128)(2,1)S(1)}, u32[]{:S(2)}, u32[]{:S(2)}) collective-permute-start(bf16[832,1152]{1,0:T(8,128)(2,1)S(1)} %get-tuple-element.19.refs_2_), channel_id=1, source_target_pairs={{0,8},{1,9},{2,10},{3,11},{4,12},{5,13},{6,14},{7,15},{8,0},{9,1},... | collective-permute-start | bytes 5750792 | tf_op jit(solution)/shard_map/ppermute | solution.py:35
  41.2 21.3 %collective-permute-start.3 = (bf16[288,1152]{1,0:T(8,128)(2,1)S(1)}, bf16[288,1152]{1,0:T(8,128)(2,1)S(1)}, u32[]{:S(2)}, u32[]{:S(2)}) collective-permute-start(bf16[288,1152]{1,0:T(8,128)(2,1)S(1)} %concatenate.24.far), channel_id=1, source_target_pairs={{0,32},{1,33},{2,34},{3,35},{4,36},{5,37},{6,38},{7,39},{8,12},{9,... | collective-permute-start | bytes 1990664 | tf_op jit(solution)/shard_map/ppermute | solution.py:35
  44.0 18.6 %collective-permute-start.1 = (bf16[288,1152]{1,0:T(8,128)(2,1)S(1)}, bf16[288,1152]{1,0:T(8,128)(2,1)S(1)}, u32[]{:S(2)}, u32[]{:S(2)}) collective-permute-start(bf16[288,1152]{1,0:T(8,128)(2,1)S(1)} %concatenate.22.near), channel_id=1, source_target_pairs={{0,4},{1,5},{2,6},{3,7},{4,0},{5,1},{6,2},{7,3},{8,40},{9,41},{10,... | collective-permute-start | bytes 1990664 | tf_op jit(solution)/shard_map/ppermute | solution.py:35
  100.8 18.4 %collective-permute-start.12 = (bf16[288,1152]{1,0:T(8,128)(2,1)}, bf16[288,1152]{1,0:T(8,128)(2,1)S(1)}, u32[]{:S(2)}, u32[]{:S(2)}) collective-permute-start(bf16[288,1152]{1,0:T(8,128)(2,1)} %get-tuple-element.29), channel_id=1, source_target_pairs={{0,2},{1,3},{2,4},{3,5},{4,6},{5,7},{6,0},{7,1},{8,24},{9,25},{10,... | collective-permute-start | bytes 1990664 | tf_op jit(solution)/shard_map/ppermute | solution.py:35
  102.4 16.7 %collective-permute-start.13 = (bf16[288,1152]{1,0:T(8,128)(2,1)}, bf16[288,1152]{1,0:T(8,128)(2,1)S(1)}, u32[]{:S(2)}, u32[]{:S(2)}) collective-permute-start(bf16[288,1152]{1,0:T(8,128)(2,1)} %get-tuple-element.30), channel_id=1, source_target_pairs={{0,6},{1,7},{2,0},{3,1},{4,2},{5,3},{6,4},{7,5},{8,56},{9,57},{10,... | collective-permute-start | bytes 1990664 | tf_op jit(solution)/shard_map/ppermute | solution.py:35
  103.5 15.7 %collective-permute-start.14 = (bf16[288,1152]{1,0:T(8,128)(2,1)}, bf16[288,1152]{1,0:T(8,128)(2,1)S(1)}, u32[]{:S(2)}, u32[]{:S(2)}) collective-permute-start(bf16[288,1152]{1,0:T(8,128)(2,1)} %get-tuple-element.31), channel_id=1, source_target_pairs={{0,4},{1,5},{2,6},{3,7},{4,0},{5,1},{6,2},{7,3},{8,40},{9,41},{10,... | collective-permute-start | bytes 1990664 | tf_op jit(solution)/shard_map/ppermute | solution.py:35
  122.5 11.2 %collective-permute-start.15 = (f32[72,1152]{1,0:T(8,128)S(1)}, f32[72,1152]{1,0:T(8,128)S(1)}, u32[]{:S(2)}, u32[]{:S(2)}) collective-permute-start(f32[72,1152]{1,0:T(8,128)S(1)} %get-tuple-element.38), channel_id=1, source_target_pairs={{0,16},{1,17},{2,18},{3,19},{4,20},{5,21},{6,22},{7,23},{8,10},{9,... | collective-permute-start | bytes 995336 | tf_op jit(solution)/shard_map/ppermute | solution.py:35
  122.7 11.0 %collective-permute-start.16 = (f32[72,1152]{1,0:T(8,128)S(1)}, f32[72,1152]{1,0:T(8,128)S(1)}, u32[]{:S(2)}, u32[]{:S(2)}) collective-permute-start(f32[72,1152]{1,0:T(8,128)S(1)} %get-tuple-element.40), channel_id=1, source_target_pairs={{0,48},{1,49},{2,50},{3,51},{4,52},{5,53},{6,54},{7,55},{8,14},{9,... | collective-permute-start | bytes 995336 | tf_op jit(solution)/shard_map/ppermute | solution.py:35
  125.3 8.5 %collective-permute-start.17 = (f32[72,1152]{1,0:T(8,128)S(1)}, f32[72,1152]{1,0:T(8,128)}, u32[]{:S(2)}, u32[]{:S(2)}) collective-permute-start(f32[72,1152]{1,0:T(8,128)S(1)} %get-tuple-element.39), channel_id=1, source_target_pairs={{0,32},{1,33},{2,34},{3,35},{4,36},{5,37},{6,38},{7,39},{8,12},{9,... | collective-permute-start | bytes 995336 | tf_op jit(solution)/shard_map/ppermute | solution.py:35
  135.7 10.1 %collective-permute-start.18 = (f32[72,1152]{1,0:T(8,128)S(1)}, f32[72,1152]{1,0:T(8,128)S(1)}, u32[]{:S(2)}, u32[]{:S(2)}) collective-permute-start(f32[72,1152]{1,0:T(8,128)S(1)} %get-tuple-element.35), channel_id=1, source_target_pairs={{0,64},{1,65},{2,66},{3,67},{4,68},{5,69},{6,70},{7,71},{8,72},{9,... | collective-permute-start | bytes 995336 | tf_op jit(solution)/shard_map/ppermute | solution.py:35
  135.8 10.0 %collective-permute-start.19 = (f32[72,1152]{1,0:T(8,128)S(1)}, f32[72,1152]{1,0:T(8,128)S(1)}, u32[]{:S(2)}, u32[]{:S(2)}) collective-permute-start(f32[72,1152]{1,0:T(8,128)S(1)} %get-tuple-element.35), channel_id=1, source_target_pairs={{0,65},{1,64},{2,67},{3,66},{4,69},{5,68},{6,71},{7,70},{8,73},{9,... | collective-permute-start | bytes 995336 | tf_op jit(solution)/shard_map/ppermute | solution.py:35
  138.5 12.8 %collective-permute-start.20 = (f32[72,1152]{1,0:T(8,128)S(1)}, f32[72,1152]{1,0:T(8,128)S(1)}, u32[]{:S(2)}, u32[]{:S(2)}) collective-permute-start(f32[72,1152]{1,0:T(8,128)S(1)} %get-tuple-element.35), channel_id=1, source_target_pairs={{0,1},{1,0},{2,3},{3,2},{4,5},{5,4},{6,7},{7,6},{8,9},{9,8},{10,11... | collective-permute-start | bytes 995336 | tf_op jit(solution)/shard_map/ppermute | solution.py:35
  161.4 18.2 %collective-permute-start.24 = (bf16[288,1152]{1,0:T(8,128)(2,1)S(1)}, bf16[288,1152]{1,0:T(8,128)(2,1)S(1)}, u32[]{:S(2)}, u32[]{:S(2)}) collective-permute-start(bf16[288,1152]{1,0:T(8,128)(2,1)S(1)} %constant_dynamic-update-slice_fusion.refs_0_), channel_id=1, source_target_pairs={{0,2},{1,3},{2,4},{3,5},{4,6},{5,7},{6,0},{7,1},{8,24},{9,25},{10,... | collective-permute-start | bytes 1990664 | tf_op jit(solution)/shard_map/ppermute | solution.py:35
  161.5 18.1 %collective-permute-start.25 = (bf16[288,1152]{1,0:T(8,128)(2,1)S(1)}, bf16[288,1152]{1,0:T(8,128)(2,1)S(1)}, u32[]{:S(2)}, u32[]{:S(2)}) collective-permute-start(bf16[288,1152]{1,0:T(8,128)(2,1)S(1)} %constant_dynamic-update-slice_fusion.refs_0_), channel_id=1, source_target_pairs={{0,6},{1,7},{2,0},{3,1},{4,2},{5,3},{6,4},{7,5},{8,56},{9,57},{10,... | collective-permute-start | bytes 1990664 | tf_op jit(solution)/shard_map/ppermute | solution.py:35
  164.1 20.4 %collective-permute-start.26 = (bf16[288,1152]{1,0:T(8,128)(2,1)S(1)}, bf16[288,1152]{1,0:T(8,128)(2,1)S(1)}, u32[]{:S(2)}, u32[]{:S(2)}) collective-permute-start(bf16[288,1152]{1,0:T(8,128)(2,1)S(1)} %constant_dynamic-update-slice_fusion.refs_0_), channel_id=1, source_target_pairs={{0,4},{1,5},{2,6},{3,7},{4,0},{5,1},{6,2},{7,3},{8,40},{9,41},{10,... | collective-permute-start | bytes 1990664 | tf_op jit(solution)/shard_map/ppermute | solution.py:35
  164.1 22.3 %collective-permute-start.27 = (bf16[288,1152]{1,0:T(8,128)(2,1)S(1)}, bf16[288,1152]{1,0:T(8,128)(2,1)S(1)}, u32[]{:S(2)}, u32[]{:S(2)}) collective-permute-start(bf16[288,1152]{1,0:T(8,128)(2,1)S(1)} %constant_dynamic-update-slice_fusion.refs_0_), channel_id=1, source_target_pairs={{0,8},{1,9},{2,10},{3,11},{4,12},{5,13},{6,14},{7,15},{8,0},{9,1},... | collective-permute-start | bytes 1990664 | tf_op jit(solution)/shard_map/ppermute | solution.py:35
  179.6 6.9 %collective-permute-start.29 = (bf16[288,1152]{1,0:T(8,128)(2,1)S(1)}, bf16[288,1152]{1,0:T(8,128)(2,1)}, u32[]{:S(2)}, u32[]{:S(2)}) collective-permute-start(bf16[288,1152]{1,0:T(8,128)(2,1)S(1)} %collective-permute-done.25.refs_2_), channel_id=1, source_target_pairs={{0,8},{1,9},{2,10},{3,11},{4,12},{5,13},{6,14},{7,15},{8,0},{9,1},... | collective-permute-start | bytes 1990664 | tf_op jit(solution)/shard_map/ppermute | solution.py:35
  (25 other events, 198.2 us)
where the time goes:
time: 195 us; the launch traced here: 194 us
  waiting for transfers between devices  63.5 us (33%)
  Pallas kernels  57.7 us (30%)
  starting transfers between devices  53.7 us (28%)
  local copies, waits for them, and re-layouts  9.05 us (5%)
  other arithmetic  7.78 us (4%)
  between operations  2.54 us (1%)
    ppermute x31, waiting for transfers between devices, send(): return lax.ppermute(value, AXES, routes(move))  63.5 us
    ppermute x31, starting transfers between devices, send(): return lax.ppermute(value, AXES, routes(move))  53.7 us
    pallas_call x1, Pallas kernels, late_pairs(): pl.pallas_call(late_kernel, grid=(4,), out_shape=[jax.ShapeDtypeStruct((2...  26.4 us
    pallas_call x1, Pallas kernels, early_pairs(): pl.pallas_call(early_kernel, grid=(3,), out_shape=jax.ShapeDtypeStruct((1...  17.1 us
    pallas_call x4, Pallas kernels, project(): pl.pallas_call(project_kernel, out_shape=[jax.ShapeDtypeStruct((832, WIDE...  8.36 us
    unnamed x36, local copies, waits for them, and re-layouts  7.51 us
    pallas_call x1, Pallas kernels, place(): pl.pallas_call(functools.partial(place_kernel, heads), out_shape=[jax.Sha...  5.85 us
  transfers between devices with their start and end apart: 31, of which 12 were waited for; matrix products, arithmetic and copies ran while one was open for 2% of the time, Pallas kernels for 12%

commit v1 on v0

--- a/solution.py
+++ b/solution.py
@@ -14,7 +14,7 @@
 F32 = jnp.float32
 WIDE = 1152
 ROWS = 2048
-VMEM_BYTES = 48 * 1024 * 1024
+VMEM_BYTES = 60 * 1024 * 1024
 
 
 def routes(move):

time: 195 us -> 188 us (0.964)
  local copies, waits for them, and re-layouts: 9.05 us -> 3.14 us
  waiting for transfers between devices: 63.5 us -> 59.1 us
  starting transfers between devices: 53.7 us -> 57.6 us
    unnamed x36 -> x26, local copies, waits for them, and re-layouts: 7.51 us -> 1.6 us
    ppermute x31, waiting for transfers between devices: 63.5 us -> 59.1 us  [send(): return lax.ppermute(value, AXES, routes(move))]
    ppermute x31, starting transfers between devices: 53.7 us -> 57.6 us  [send(): return lax.ppermute(value, AXES, routes(move))]
  transfers between devices with their start and end apart: 31 -> 31, of which waited for: 12 -> 14; matrix products, arithmetic and copies ran while one was open for 2% -> 2% of each run, Pallas kernels for 12% -> 12%
where the time goes in v1:
time: 188 us
  waiting for transfers between devices  59.1 us (31%)
  Pallas kernels  58 us (31%)
  starting transfers between devices  57.6 us (31%)
  other arithmetic  7.83 us (4%)
  local copies, waits for them, and re-layouts  3.14 us (2%)
  between operations  2.53 us (1%)
    ppermute x31, waiting for transfers between devices, send(): return lax.ppermute(value, AXES, routes(move))  59.1 us
    ppermute x31, starting transfers between devices, send(): return lax.ppermute(value, AXES, routes(move))  57.6 us
    pallas_call x1, Pallas kernels, late_pairs(): pl.pallas_call(late_kernel, grid=(4,), out_shape=[jax.ShapeDtypeStruct((2...  26.7 us
    pallas_call x1, Pallas kernels, early_pairs(): pl.pallas_call(early_kernel, grid=(3,), out_shape=jax.ShapeDtypeStruct((1...  17.1 us
    pallas_call x4, Pallas kernels, project(): pl.pallas_call(project_kernel, out_shape=[jax.ShapeDtypeStruct((832, WIDE...  8.36 us
    pallas_call x1, Pallas kernels, place(): pl.pallas_call(functools.partial(place_kernel, heads), out_shape=[jax.Sha...  5.85 us
  transfers between devices with their start and end apart: 31, of which 14 were waited for; matrix products, arithmetic and copies ran while one was open for 2% of the time, Pallas kernels for 12%

profile of v1, /device:TPU:1, one launch (start us, length us, event | category | flops | bytes accessed | tf_op | source)
XLA Modules:
  0.0 188.2 jit_solution(4862044085104559662)
XLA Ops:
  2.5 2.5 %collective-permute-start.2 = (bf16[144,1152]{1,0:T(8,128)(2,1)S(1)}, bf16[144,1152]{1,0:T(8,128)(2,1)S(1)}, u32[]{:S(2)}, u32[]{:S(2)}) collective-permute-start(bf16[144,1152]{1,0:T(8,128)(2,1)S(1)} %get-tuple-element.43), channel_id=1, source_target_pairs={{0,65},{1,64},{2,67},{3,66},{4,69},{5,68},{6,71},{7,70},{8,72},{9,... | collective-permute-start | bytes 995336 | tf_op jit(solution)/shard_map/ppermute | solution.py:35
  7.3 2.6 %collective-permute-done.2 = bf16[144,1152]{1,0:T(8,128)(2,1)S(1)} collective-permute-done((bf16[144,1152]{1,0:T(8,128)(2,1)S(1)}, bf16[144,1152]{1,0:T(8,128)(2,1)S(1)}, u32[]{:S(2)}, u32[]{:S(2)}) %collective-permute-start.2) | collective-permute-done | bytes 331808 | tf_op jit(solution)/shard_map/ppermute | solution.py:35
  10.4 2.5 %collective-permute-start.7 = (bf16[288,1152]{1,0:T(8,128)(2,1)S(1)}, bf16[288,1152]{1,0:T(8,128)(2,1)S(1)}, u32[]{:S(2)}, u32[]{:S(2)}) collective-permute-start(bf16[288,1152]{1,0:T(8,128)(2,1)S(1)} %concatenate.24.far), channel_id=1, source_target_pairs={{0,48},{1,49},{2,50},{3,51},{4,52},{5,53},{6,54},{7,55},{8,14},{9,... | collective-permute-start | bytes 1990664 | tf_op jit(solution)/shard_map/ppermute | solution.py:35
  13.0 2.8 %collective-permute-done = bf16[144,1152]{1,0:T(8,128)(2,1)S(1)} collective-permute-done((bf16[144,1152]{1,0:T(8,128)(2,1)S(1)}, bf16[144,1152]{1,0:T(8,128)(2,1)S(1)}, u32[]{:S(2)}, u32[]{:S(2)}) %collective-permute-start) | collective-permute-done | bytes 331808 | tf_op jit(solution)/shard_map/ppermute | solution.py:35
  16.3 2.8 %collective-permute-start.6 = (bf16[288,1152]{1,0:T(8,128)(2,1)S(1)}, bf16[288,1152]{1,0:T(8,128)(2,1)S(1)}, u32[]{:S(2)}, u32[]{:S(2)}) collective-permute-start(bf16[288,1152]{1,0:T(8,128)(2,1)S(1)} %concatenate.22.near), channel_id=1, source_target_pairs={{0,6},{1,7},{2,0},{3,1},{4,2},{5,3},{6,4},{7,5},{8,56},{9,57},{10,... | collective-permute-start | bytes 1990664 | tf_op jit(solution)/shard_map/ppermute | solution.py:35
  19.1 3.0 %broadcast_select_fusion = (bf16[1152,1152]{1,0:T(8,128)(2,1)S(1)}, bf16[1152,1152]{1,0:T(8,128)(2,1)S(1)}) fusion(bf16[1152,1152]{1,0:T(8,128)(2,1)} %param.10, bf16[1152,1152]{1,0:T(8,128)(2,1)} %param.9, pred[]{:T(512)S(6)} %eq.5), kind=kLoop, calls=%fused_computation | loop fusion | flops 2654208 | bytes 10616833 | tf_op jit(solution)/shard_map/jit(_where)/select_n | solution.py:404
  24.3 4.4 %collective-permute-start.8 = (bf16[832,1152]{1,0:T(8,128)(2,1)S(1)}, bf16[832,1152]{1,0:T(8,128)(2,1)S(1)}, u32[]{:S(2)}, u32[]{:S(2)}) collective-permute-start(bf16[832,1152]{1,0:T(8,128)(2,1)S(1)} %get-tuple-element.17.refs_0_), channel_id=1, source_target_pairs={{0,8},{1,9},{2,10},{3,11},{4,12},{5,13},{6,14},{7,15},{8,0},{9,1},... | collective-permute-start | bytes 5750792 | tf_op jit(solution)/shard_map/ppermute | solution.py:35
  28.7 4.0 %collective-permute-done.6.near = bf16[288,1152]{1,0:T(8,128)(2,1)S(1)} collective-permute-done((bf16[288,1152]{1,0:T(8,128)(2,1)S(1)}, bf16[288,1152]{1,0:T(8,128)(2,1)S(1)}, u32[]{:S(2)}, u32[]{:S(2)}) %collective-permute-start.6) | collective-permute-done | bytes 663584 | tf_op jit(solution)/shard_map/ppermute | solution.py:35
  41.2 2.8 %collective-permute-start.3 = (bf16[288,1152]{1,0:T(8,128)(2,1)S(1)}, bf16[288,1152]{1,0:T(8,128)(2,1)S(1)}, u32[]{:S(2)}, u32[]{:S(2)}) collective-permute-start(bf16[288,1152]{1,0:T(8,128)(2,1)S(1)} %concatenate.24.far), channel_id=1, source_target_pairs={{0,32},{1,33},{2,34},{3,35},{4,36},{5,37},{6,38},{7,39},{8,12},{9,... | collective-permute-start | bytes 1990664 | tf_op jit(solution)/shard_map/ppermute | solution.py:35
  45.4 17.1 %early_pairs.1.early = f32[1536,1152]{1,0:T(8,128)} custom-call(f32[3]{0:T(128)S(1)} %pad_maximum_fusion.5.knob_ref, bf16[832,1152]{1,0:T(8,128)(2,1)S(1)} %get-tuple-element.17.refs_0_, bf16[832,1152]{1,0:T(8,128)(2,1)S(1)} %get-tuple-element.18.refs_1_, bf16[832,1152]{1,0:T(8,128)(2,1)S(1)} %get-tuple-element.19.refs_2_, ...), custom_call_target="tpu_custom_call" | custom-call | flops 10871635968 | bytes 14000000 | tf_op jit(solution)/shard_map/early_pairs/pallas_call | solution.py:195
  66.5 3.7 %collective-permute-done.11.refs_7_ = bf16[832,1152]{1,0:T(8,128)(2,1)} collective-permute-done((bf16[832,1152]{1,0:T(8,128)(2,1)S(1)}, bf16[832,1152]{1,0:T(8,128)(2,1)}, u32[]{:S(2)}, u32[]{:S(2)}) %collective-permute-start.11) | collective-permute-done | bytes 1916960 | tf_op jit(solution)/shard_map/ppermute | solution.py:35
  70.2 26.7 %late_pairs.1 = (f32[288,1152]{1,0:T(8,128)}, bf16[288,1152]{1,0:T(8,128)(2,1)}, bf16[288,1152]{1,0:T(8,128)(2,1)}, bf16[288,1152]{1,0:T(8,128)(2,1)}) custom-call(s32[1]{0:T(128)} %bitcast.9.at_ref, f32[3]{0:T(128)} %copy-done, f32[1536,1152]{1,0:T(8,128)} %early_pairs.1.early, bf16[832,1152]{1,0:T(8,128)(2,1)} %copy-done.1, bf16[832,1152]{1,0:T(8,128)(2,1)} %copy-done.5, ...), custom_call_target="tpu_custom_call" | custom-call | flops 13891534848 | bytes 25000000 | tf_op jit(solution)/shard_map/late_pairs/pallas_call | solution.py:294
  100.4 14.9 %collective-permute-done.12 = bf16[288,1152]{1,0:T(8,128)(2,1)S(1)} collective-permute-done((bf16[288,1152]{1,0:T(8,128)(2,1)}, bf16[288,1152]{1,0:T(8,128)(2,1)S(1)}, u32[]{:S(2)}, u32[]{:S(2)}) %collective-permute-start.12) | collective-permute-done | bytes 663584 | tf_op jit(solution)/shard_map/ppermute | solution.py:35
  117.5 2.5 %collective-permute-start.16 = (f32[72,1152]{1,0:T(8,128)S(1)}, f32[72,1152]{1,0:T(8,128)S(1)}, u32[]{:S(2)}, u32[]{:S(2)}) collective-permute-start(f32[72,1152]{1,0:T(8,128)S(1)} %get-tuple-element.40), channel_id=1, source_target_pairs={{0,48},{1,49},{2,50},{3,51},{4,52},{5,53},{6,54},{7,55},{8,14},{9,... | collective-permute-start | bytes 995336 | tf_op jit(solution)/shard_map/ppermute | solution.py:35
  120.0 8.5 %collective-permute-done.15 = f32[72,1152]{1,0:T(8,128)S(1)} collective-permute-done((f32[72,1152]{1,0:T(8,128)S(1)}, f32[72,1152]{1,0:T(8,128)S(1)}, u32[]{:S(2)}, u32[]{:S(2)}) %collective-permute-start.15) | collective-permute-done | bytes 331808 | tf_op jit(solution)/shard_map/ppermute | solution.py:35
  130.6 2.6 %collective-permute-start.19 = (f32[72,1152]{1,0:T(8,128)S(1)}, f32[72,1152]{1,0:T(8,128)S(1)}, u32[]{:S(2)}, u32[]{:S(2)}) collective-permute-start(f32[72,1152]{1,0:T(8,128)S(1)} %get-tuple-element.35), channel_id=1, source_target_pairs={{0,65},{1,64},{2,67},{3,66},{4,69},{5,68},{6,71},{7,70},{8,73},{9,... | collective-permute-start | bytes 995336 | tf_op jit(solution)/shard_map/ppermute | solution.py:35
  133.9 5.8 %collective-permute-done.18 = f32[72,1152]{1,0:T(8,128)S(1)} collective-permute-done((f32[72,1152]{1,0:T(8,128)S(1)}, f32[72,1152]{1,0:T(8,128)S(1)}, u32[]{:S(2)}, u32[]{:S(2)}) %collective-permute-start.18) | collective-permute-done | bytes 331808 | tf_op jit(solution)/shard_map/ppermute | solution.py:35
  139.8 7.0 %collective-permute-done.20 = f32[72,1152]{1,0:T(8,128)S(1)} collective-permute-done((f32[72,1152]{1,0:T(8,128)S(1)}, f32[72,1152]{1,0:T(8,128)S(1)}, u32[]{:S(2)}, u32[]{:S(2)}) %collective-permute-start.20) | collective-permute-done | bytes 331808 | tf_op jit(solution)/shard_map/ppermute | solution.py:35
  152.7 3.0 %collective-permute-done.23 = bf16[72,1152]{1,0:T(8,128)(2,1)S(1)} collective-permute-done((bf16[72,1152]{1,0:T(8,128)(2,1)S(1)}, bf16[72,1152]{1,0:T(8,128)(2,1)S(1)}, u32[]{:S(2)}, u32[]{:S(2)}) %collective-permute-start.23) | collective-permute-done | bytes 165920 | tf_op jit(solution)/shard_map/ppermute | solution.py:35
  155.8 2.8 %collective-permute-start.25 = (bf16[288,1152]{1,0:T(8,128)(2,1)S(1)}, bf16[288,1152]{1,0:T(8,128)(2,1)S(1)}, u32[]{:S(2)}, u32[]{:S(2)}) collective-permute-start(bf16[288,1152]{1,0:T(8,128)(2,1)S(1)} %constant_dynamic-update-slice_fusion.refs_0_), channel_id=1, source_target_pairs={{0,6},{1,7},{2,0},{3,1},{4,2},{5,3},{6,4},{7,5},{8,56},{9,57},{10,... | collective-permute-start | bytes 1990664 | tf_op jit(solution)/shard_map/ppermute | solution.py:35
  159.7 4.8 %collective-permute-start.27 = (bf16[288,1152]{1,0:T(8,128)(2,1)S(1)}, bf16[288,1152]{1,0:T(8,128)(2,1)S(1)}, u32[]{:S(2)}, u32[]{:S(2)}) collective-permute-start(bf16[288,1152]{1,0:T(8,128)(2,1)S(1)} %constant_dynamic-update-slice_fusion.refs_0_), channel_id=1, source_target_pairs={{0,8},{1,9},{2,10},{3,11},{4,12},{5,13},{6,14},{7,15},{8,0},{9,1},... | collective-permute-start | bytes 1990664 | tf_op jit(solution)/shard_map/ppermute | solution.py:35
  166.9 5.2 %collective-permute-start.28 = (bf16[288,1152]{1,0:T(8,128)(2,1)S(1)}, bf16[288,1152]{1,0:T(8,128)(2,1)}, u32[]{:S(2)}, u32[]{:S(2)}) collective-permute-start(bf16[288,1152]{1,0:T(8,128)(2,1)S(1)} %collective-permute-done.24.refs_1_), channel_id=1, source_target_pairs={{0,8},{1,9},{2,10},{3,11},{4,12},{5,13},{6,14},{7,15},{8,0},{9,1},... | collective-permute-start | bytes 1990664 | tf_op jit(solution)/shard_map/ppermute | solution.py:35
  173.3 5.4 %collective-permute-start.29 = (bf16[288,1152]{1,0:T(8,128)(2,1)S(1)}, bf16[288,1152]{1,0:T(8,128)(2,1)}, u32[]{:S(2)}, u32[]{:S(2)}) collective-permute-start(bf16[288,1152]{1,0:T(8,128)(2,1)S(1)} %collective-permute-done.25.refs_2_), channel_id=1, source_target_pairs={{0,8},{1,9},{2,10},{3,11},{4,12},{5,13},{6,14},{7,15},{8,0},{9,1},... | collective-permute-start | bytes 1990664 | tf_op jit(solution)/shard_map/ppermute | solution.py:35
  182.1 5.8 %place.1 = (f32[1152,1152]{1,0:T(8,128)}, f32[1152,1152]{1,0:T(8,128)}) custom-call(s32[9]{0:T(128)S(1)} %stack.45.where_ref, bf16[288,1152]{1,0:T(8,128)(2,1)S(1)} %constant_dynamic-update-slice_fusion.refs_0_, bf16[288,1152]{1,0:T(8,128)(2,1)S(1)} %collective-permute-done.24.refs_1_, bf16[288,1152]{1,0:T(8,128)(2,1)S(1)} %collective-permute-done.25.refs_2_, ...), custom_call_target="tpu_custom_call" | custom-call | tf_op jit(solution)/shard_map/place/pallas_call | solution.py:359
  (99 shorter events, 42.5 us)
Async XLA Ops:
  2.5 7.3 %collective-permute-start.2 = (bf16[144,1152]{1,0:T(8,128)(2,1)S(1)}, bf16[144,1152]{1,0:T(8,128)(2,1)S(1)}, u32[]{:S(2)}, u32[]{:S(2)}) collective-permute-start(bf16[144,1152]{1,0:T(8,128)(2,1)S(1)} %get-tuple-element.43), channel_id=1, source_target_pairs={{0,65},{1,64},{2,67},{3,66},{4,69},{5,68},{6,71},{7,70},{8,72},{9,... | collective-permute-start | bytes 995336 | tf_op jit(solution)/shard_map/ppermute | solution.py:35
  5.1 10.7 %collective-permute-start = (bf16[144,1152]{1,0:T(8,128)(2,1)S(1)}, bf16[144,1152]{1,0:T(8,128)(2,1)S(1)}, u32[]{:S(2)}, u32[]{:S(2)}) collective-permute-start(bf16[144,1152]{1,0:T(8,128)(2,1)S(1)} %get-tuple-element.44), channel_id=1, source_target_pairs={{0,64},{1,65},{2,66},{3,67},{4,68},{5,69},{6,70},{7,71},{8,73},{9,... | collective-permute-start | bytes 995336 | tf_op jit(solution)/shard_map/ppermute | solution.py:35
  10.4 18.3 %collective-permute-start.7 = (bf16[288,1152]{1,0:T(8,128)(2,1)S(1)}, bf16[288,1152]{1,0:T(8,128)(2,1)S(1)}, u32[]{:S(2)}, u32[]{:S(2)}) collective-permute-start(bf16[288,1152]{1,0:T(8,128)(2,1)S(1)} %concatenate.24.far), channel_id=1, source_target_pairs={{0,48},{1,49},{2,50},{3,51},{4,52},{5,53},{6,54},{7,55},{8,14},{9,... | collective-permute-start | bytes 1990664 | tf_op jit(solution)/shard_map/ppermute | solution.py:35
  13.0 23.5 %collective-permute-start.5 = (bf16[288,1152]{1,0:T(8,128)(2,1)S(1)}, bf16[288,1152]{1,0:T(8,128)(2,1)S(1)}, u32[]{:S(2)}, u32[]{:S(2)}) collective-permute-start(bf16[288,1152]{1,0:T(8,128)(2,1)S(1)} %concatenate.24.far), channel_id=1, source_target_pairs={{0,16},{1,17},{2,18},{3,19},{4,20},{5,21},{6,22},{7,23},{8,10},{9,... | collective-permute-start | bytes 1990664 | tf_op jit(solution)/shard_map/ppermute | solution.py:35
  16.3 16.3 %collective-permute-start.6 = (bf16[288,1152]{1,0:T(8,128)(2,1)S(1)}, bf16[288,1152]{1,0:T(8,128)(2,1)S(1)}, u32[]{:S(2)}, u32[]{:S(2)}) collective-permute-start(bf16[288,1152]{1,0:T(8,128)(2,1)S(1)} %concatenate.22.near), channel_id=1, source_target_pairs={{0,6},{1,7},{2,0},{3,1},{4,2},{5,3},{6,4},{7,5},{8,56},{9,57},{10,... | collective-permute-start | bytes 1990664 | tf_op jit(solution)/shard_map/ppermute | solution.py:35
  19.1 17.4 %collective-permute-start.4 = (bf16[288,1152]{1,0:T(8,128)(2,1)S(1)}, bf16[288,1152]{1,0:T(8,128)(2,1)S(1)}, u32[]{:S(2)}, u32[]{:S(2)}) collective-permute-start(bf16[288,1152]{1,0:T(8,128)(2,1)S(1)} %concatenate.22.near), channel_id=1, source_target_pairs={{0,2},{1,3},{2,4},{3,5},{4,6},{5,7},{6,0},{7,1},{8,24},{9,25},{10,... | collective-permute-start | bytes 1990664 | tf_op jit(solution)/shard_map/ppermute | solution.py:35
  24.3 21.0 %collective-permute-start.8 = (bf16[832,1152]{1,0:T(8,128)(2,1)S(1)}, bf16[832,1152]{1,0:T(8,128)(2,1)S(1)}, u32[]{:S(2)}, u32[]{:S(2)}) collective-permute-start(bf16[832,1152]{1,0:T(8,128)(2,1)S(1)} %get-tuple-element.17.refs_0_), channel_id=1, source_target_pairs={{0,8},{1,9},{2,10},{3,11},{4,12},{5,13},{6,14},{7,15},{8,0},{9,1},... | collective-permute-start | bytes 5750792 | tf_op jit(solution)/shard_map/ppermute | solution.py:35
  34.8 10.5 %collective-permute-start.10 = (bf16[832,1152]{1,0:T(8,128)(2,1)S(1)}, bf16[832,1152]{1,0:T(8,128)(2,1)S(1)}, u32[]{:S(2)}, u32[]{:S(2)}) collective-permute-start(bf16[832,1152]{1,0:T(8,128)(2,1)S(1)} %get-tuple-element.19.refs_2_), channel_id=1, source_target_pairs={{0,8},{1,9},{2,10},{3,11},{4,12},{5,13},{6,14},{7,15},{8,0},{9,1},... | collective-permute-start | bytes 5750792 | tf_op jit(solution)/shard_map/ppermute | solution.py:35
  41.2 21.3 %collective-permute-start.3 = (bf16[288,1152]{1,0:T(8,128)(2,1)S(1)}, bf16[288,1152]{1,0:T(8,128)(2,1)S(1)}, u32[]{:S(2)}, u32[]{:S(2)}) collective-permute-start(bf16[288,1152]{1,0:T(8,128)(2,1)S(1)} %concatenate.24.far), channel_id=1, source_target_pairs={{0,32},{1,33},{2,34},{3,35},{4,36},{5,37},{6,38},{7,39},{8,12},{9,... | collective-permute-start | bytes 1990664 | tf_op jit(solution)/shard_map/ppermute | solution.py:35
  44.0 18.6 %collective-permute-start.1 = (bf16[288,1152]{1,0:T(8,128)(2,1)S(1)}, bf16[288,1152]{1,0:T(8,128)(2,1)S(1)}, u32[]{:S(2)}, u32[]{:S(2)}) collective-permute-start(bf16[288,1152]{1,0:T(8,128)(2,1)S(1)} %concatenate.22.near), channel_id=1, source_target_pairs={{0,4},{1,5},{2,6},{3,7},{4,0},{5,1},{6,2},{7,3},{8,40},{9,41},{10,... | collective-permute-start | bytes 1990664 | tf_op jit(solution)/shard_map/ppermute | solution.py:35
  96.9 18.4 %collective-permute-start.12 = (bf16[288,1152]{1,0:T(8,128)(2,1)}, bf16[288,1152]{1,0:T(8,128)(2,1)S(1)}, u32[]{:S(2)}, u32[]{:S(2)}) collective-permute-start(bf16[288,1152]{1,0:T(8,128)(2,1)} %get-tuple-element.29), channel_id=1, source_target_pairs={{0,2},{1,3},{2,4},{3,5},{4,6},{5,7},{6,0},{7,1},{8,24},{9,25},{10,... | collective-permute-start | bytes 1990664 | tf_op jit(solution)/shard_map/ppermute | solution.py:35
  98.6 16.7 %collective-permute-start.13 = (bf16[288,1152]{1,0:T(8,128)(2,1)}, bf16[288,1152]{1,0:T(8,128)(2,1)S(1)}, u32[]{:S(2)}, u32[]{:S(2)}) collective-permute-start(bf16[288,1152]{1,0:T(8,128)(2,1)} %get-tuple-element.30), channel_id=1, source_target_pairs={{0,6},{1,7},{2,0},{3,1},{4,2},{5,3},{6,4},{7,5},{8,56},{9,57},{10,... | collective-permute-start | bytes 1990664 | tf_op jit(solution)/shard_map/ppermute | solution.py:35
  99.6 15.7 %collective-permute-start.14 = (bf16[288,1152]{1,0:T(8,128)(2,1)}, bf16[288,1152]{1,0:T(8,128)(2,1)S(1)}, u32[]{:S(2)}, u32[]{:S(2)}) collective-permute-start(bf16[288,1152]{1,0:T(8,128)(2,1)} %get-tuple-element.31), channel_id=1, source_target_pairs={{0,4},{1,5},{2,6},{3,7},{4,0},{5,1},{6,2},{7,3},{8,40},{9,41},{10,... | collective-permute-start | bytes 1990664 | tf_op jit(solution)/shard_map/ppermute | solution.py:35
  117.0 11.4 %collective-permute-start.15 = (f32[72,1152]{1,0:T(8,128)S(1)}, f32[72,1152]{1,0:T(8,128)S(1)}, u32[]{:S(2)}, u32[]{:S(2)}) collective-permute-start(f32[72,1152]{1,0:T(8,128)S(1)} %get-tuple-element.38), channel_id=1, source_target_pairs={{0,16},{1,17},{2,18},{3,19},{4,20},{5,21},{6,22},{7,23},{8,10},{9,... | collective-permute-start | bytes 995336 | tf_op jit(solution)/shard_map/ppermute | solution.py:35
  117.5 11.0 %collective-permute-start.16 = (f32[72,1152]{1,0:T(8,128)S(1)}, f32[72,1152]{1,0:T(8,128)S(1)}, u32[]{:S(2)}, u32[]{:S(2)}) collective-permute-start(f32[72,1152]{1,0:T(8,128)S(1)} %get-tuple-element.40), channel_id=1, source_target_pairs={{0,48},{1,49},{2,50},{3,51},{4,52},{5,53},{6,54},{7,55},{8,14},{9,... | collective-permute-start | bytes 995336 | tf_op jit(solution)/shard_map/ppermute | solution.py:35
  120.0 8.5 %collective-permute-start.17 = (f32[72,1152]{1,0:T(8,128)S(1)}, f32[72,1152]{1,0:T(8,128)}, u32[]{:S(2)}, u32[]{:S(2)}) collective-permute-start(f32[72,1152]{1,0:T(8,128)S(1)} %get-tuple-element.39), channel_id=1, source_target_pairs={{0,32},{1,33},{2,34},{3,35},{4,36},{5,37},{6,38},{7,39},{8,12},{9,... | collective-permute-start | bytes 995336 | tf_op jit(solution)/shard_map/ppermute | solution.py:35
  130.5 9.2 %collective-permute-start.18 = (f32[72,1152]{1,0:T(8,128)S(1)}, f32[72,1152]{1,0:T(8,128)S(1)}, u32[]{:S(2)}, u32[]{:S(2)}) collective-permute-start(f32[72,1152]{1,0:T(8,128)S(1)} %get-tuple-element.35), channel_id=1, source_target_pairs={{0,64},{1,65},{2,66},{3,67},{4,68},{5,69},{6,70},{7,71},{8,72},{9,... | collective-permute-start | bytes 995336 | tf_op jit(solution)/shard_map/ppermute | solution.py:35
  130.6 9.2 %collective-permute-start.19 = (f32[72,1152]{1,0:T(8,128)S(1)}, f32[72,1152]{1,0:T(8,128)S(1)}, u32[]{:S(2)}, u32[]{:S(2)}) collective-permute-start(f32[72,1152]{1,0:T(8,128)S(1)} %get-tuple-element.35), channel_id=1, source_target_pairs={{0,65},{1,64},{2,67},{3,66},{4,69},{5,68},{6,71},{7,70},{8,73},{9,... | collective-permute-start | bytes 995336 | tf_op jit(solution)/shard_map/ppermute | solution.py:35
  133.2 13.5 %collective-permute-start.20 = (f32[72,1152]{1,0:T(8,128)S(1)}, f32[72,1152]{1,0:T(8,128)S(1)}, u32[]{:S(2)}, u32[]{:S(2)}) collective-permute-start(f32[72,1152]{1,0:T(8,128)S(1)} %get-tuple-element.35), channel_id=1, source_target_pairs={{0,1},{1,0},{2,3},{3,2},{4,5},{5,4},{6,7},{7,6},{8,9},{9,8},{10,11... | collective-permute-start | bytes 995336 | tf_op jit(solution)/shard_map/ppermute | solution.py:35
  155.8 11.1 %collective-permute-start.24 = (bf16[288,1152]{1,0:T(8,128)(2,1)S(1)}, bf16[288,1152]{1,0:T(8,128)(2,1)S(1)}, u32[]{:S(2)}, u32[]{:S(2)}) collective-permute-start(bf16[288,1152]{1,0:T(8,128)(2,1)S(1)} %constant_dynamic-update-slice_fusion.refs_0_), channel_id=1, source_target_pairs={{0,2},{1,3},{2,4},{3,5},{4,6},{5,7},{6,0},{7,1},{8,24},{9,25},{10,... | collective-permute-start | bytes 1990664 | tf_op jit(solution)/shard_map/ppermute | solution.py:35
  155.8 17.5 %collective-permute-start.25 = (bf16[288,1152]{1,0:T(8,128)(2,1)S(1)}, bf16[288,1152]{1,0:T(8,128)(2,1)S(1)}, u32[]{:S(2)}, u32[]{:S(2)}) collective-permute-start(bf16[288,1152]{1,0:T(8,128)(2,1)S(1)} %constant_dynamic-update-slice_fusion.refs_0_), channel_id=1, source_target_pairs={{0,6},{1,7},{2,0},{3,1},{4,2},{5,3},{6,4},{7,5},{8,56},{9,57},{10,... | collective-permute-start | bytes 1990664 | tf_op jit(solution)/shard_map/ppermute | solution.py:35
  158.6 20.1 %collective-permute-start.26 = (bf16[288,1152]{1,0:T(8,128)(2,1)S(1)}, bf16[288,1152]{1,0:T(8,128)(2,1)S(1)}, u32[]{:S(2)}, u32[]{:S(2)}) collective-permute-start(bf16[288,1152]{1,0:T(8,128)(2,1)S(1)} %constant_dynamic-update-slice_fusion.refs_0_), channel_id=1, source_target_pairs={{0,4},{1,5},{2,6},{3,7},{4,0},{5,1},{6,2},{7,3},{8,40},{9,41},{10,... | collective-permute-start | bytes 1990664 | tf_op jit(solution)/shard_map/ppermute | solution.py:35
  159.7 20.7 %collective-permute-start.27 = (bf16[288,1152]{1,0:T(8,128)(2,1)S(1)}, bf16[288,1152]{1,0:T(8,128)(2,1)S(1)}, u32[]{:S(2)}, u32[]{:S(2)}) collective-permute-start(bf16[288,1152]{1,0:T(8,128)(2,1)S(1)} %constant_dynamic-update-slice_fusion.refs_0_), channel_id=1, source_target_pairs={{0,8},{1,9},{2,10},{3,11},{4,12},{5,13},{6,14},{7,15},{8,0},{9,1},... | collective-permute-start | bytes 1990664 | tf_op jit(solution)/shard_map/ppermute | solution.py:35
  166.9 13.5 %collective-permute-start.28 = (bf16[288,1152]{1,0:T(8,128)(2,1)S(1)}, bf16[288,1152]{1,0:T(8,128)(2,1)}, u32[]{:S(2)}, u32[]{:S(2)}) collective-permute-start(bf16[288,1152]{1,0:T(8,128)(2,1)S(1)} %collective-permute-done.24.refs_1_), channel_id=1, source_target_pairs={{0,8},{1,9},{2,10},{3,11},{4,12},{5,13},{6,14},{7,15},{8,0},{9,1},... | collective-permute-start | bytes 1990664 | tf_op jit(solution)/shard_map/ppermute | solution.py:35
  (20 other events, 211.5 us)

commit v2 on v1

--- a/solution.py
+++ b/solution.py
@@ -324,53 +324,40 @@
     )(at, knobs, early, *own, *over, *own_rows)
 
 
-def place_kernel(heads, where_ref, *refs):
-    count = len(heads)
-    pieces, outs = refs[:count], refs[-6:-4]
-    narrow, wide, in_sems, out_sems = refs[-4:]
-    loads = [
-        pltpu.make_async_copy(piece, narrow.at[i], in_sems.at[i]) for i, piece in enumerate(pieces)
-    ]
-    for load in loads:
-        load.start()
+def place_kernel(*refs):
+    pieces, outs = refs[:8], refs[8:10]
+    wide, sems = refs[10:]
+    core, at_x, at_y = (lax.axis_index(axis) for axis in ("c", "x", "y"))
 
     def stores(i):
-        head = where_ref[0] if heads[i] == 0 else 1 - where_ref[0]
-        row = pl.multiple_of(where_ref[1 + i] * 288, 288)
+        mine = i < 4
+        head = core if mine else 1 - core
+        at = jnp.where(head == 0, at_x, at_y)
+        row = pl.multiple_of(lax.rem(at + 4 - (0, 1, 3, 2)[i % 4], 4) * 288, 288)
         for h in range(2):
-            copy = pltpu.make_async_copy(
-                wide.at[i], outs[h].at[pl.ds(row, 288), :], out_sems.at[i]
-            )
+            copy = pltpu.make_async_copy(wide.at[i], outs[h].at[pl.ds(row, 288), :], sems.at[i])
             yield head == h, copy
 
-    for i in range(count):
-        loads[i].wait()
-        wide[i] = narrow[i].astype(F32)
+    for i in (0, 4, 1, 5, 2, 6, 3, 7):
+        wide[i] = pieces[i][...].astype(F32)
         for here, copy in stores(i):
             pl.when(here)(copy.start)
-    for i in range(count):
+    for i in range(8):
         for here, copy in stores(i):
             pl.when(here)(copy.wait)
 
 
-def place(where, heads, pieces, held):
-    count = len(pieces)
-    hbm = pl.BlockSpec(memory_space=pl.ANY)
+def place(pieces):
+    anywhere = pl.BlockSpec(memory_space=pl.ANY)
     return pl.pallas_call(
-        functools.partial(place_kernel, heads),
+        place_kernel,
         out_shape=[jax.ShapeDtypeStruct((WIDE, WIDE), F32)] * 2,
-        in_specs=[pl.BlockSpec(memory_space=pltpu.SMEM)] + [hbm] * (count + len(held)),
-        out_specs=[hbm] * 2,
-        input_output_aliases={1 + count + i: i for i in range(len(held))},
-        scratch_shapes=[
-            pltpu.VMEM((count, 288, WIDE), BF16),
-            pltpu.VMEM((count, 288, WIDE), F32),
-            pltpu.SemaphoreType.DMA((count,)),
-            pltpu.SemaphoreType.DMA((count,)),
-        ],
-        compiler_params=pltpu.CompilerParams(vmem_limit_bytes=32 * 1024 * 1024),
+        in_specs=[pl.BlockSpec(memory_space=pltpu.VMEM)] * 8,
+        out_specs=[anywhere] * 2,
+        scratch_shapes=[pltpu.VMEM((8, 288, WIDE), F32), pltpu.SemaphoreType.DMA((8,))],
+        compiler_params=pltpu.CompilerParams(vmem_limit_bytes=16 * 1024 * 1024),
         name="place",
-    )(where, *pieces, *held)
+    )(*pieces)
 
 
 def added(total, parts):
@@ -445,17 +432,9 @@
         quarter = lax.dynamic_update_slice_in_dim(
             quarter, piece, lax.rem(at_second + 4 - by, 4) * 72, 0
         )
-    core = lax.axis_index("c")
-
-    def where(bys):
-        places = [lax.rem(at + 4 - by, 4) for at in (at_first, at_second) for by in bys]
-        return jnp.stack([core] + places).astype(jnp.int32)
-
     pieces = [quarter] + [send(quarter, ring(by, 0)) for by in (1, 3, 2)]
     pieces = pieces + [send(piece, other_core) for piece in pieces]
-    places = [lax.rem(at + 4 - by, 4) for at in (at_first, at_second) for by in (0, 1, 3, 2)]
-    where = jnp.stack([lax.axis_index("c")] + places).astype(jnp.int32)
-    return tuple(place(where, (0, 0, 0, 0, 1, 1, 1, 1), pieces, ()))
+    return tuple(place(pieces))
 
 
 def solution(mesh):

time: 188 us -> 187 us (level)
  no operation moved by 1% of the time
where the time goes in v2:
time: 187 us
  waiting for transfers between devices  59.1 us (32%)
  starting transfers between devices  57.5 us (31%)
  Pallas kernels  56.3 us (30%)
  other arithmetic  7.7 us (4%)
  local copies, waits for them, and re-layouts  3.96 us (2%)
  between operations  2.53 us (1%)
    ppermute x31, waiting for transfers between devices, send(): return lax.ppermute(value, AXES, routes(move))  59.1 us
    ppermute x31, starting transfers between devices, send(): return lax.ppermute(value, AXES, routes(move))  57.5 us
    pallas_call x1, Pallas kernels, late_pairs(): pl.pallas_call(late_kernel, grid=(4,), out_shape=[jax.ShapeDtypeStruct((2...  26.7 us
    pallas_call x1, Pallas kernels, early_pairs(): pl.pallas_call(early_kernel, grid=(3,), out_shape=jax.ShapeDtypeStruct((1...  17.1 us
    pallas_call x4, Pallas kernels, project(): pl.pallas_call(project_kernel, out_shape=[jax.ShapeDtypeStruct((832, WIDE...  8.36 us
    pallas_call x1, Pallas kernels, place(): pl.pallas_call(place_kernel, out_shape=[jax.ShapeDtypeStruct((WIDE, WIDE)...  4.16 us
  transfers between devices with their start and end apart: 31, of which 14 were waited for; matrix products, arithmetic and copies ran while one was open for 2% of the time, Pallas kernels for 12%

profile of v2, /device:TPU:1, one launch (start us, length us, event | category | flops | bytes accessed | tf_op | source)
XLA Modules:
  0.0 187.1 jit_solution(9826760790118944582)
XLA Ops:
  2.5 2.5 %collective-permute-start.2 = (bf16[144,1152]{1,0:T(8,128)(2,1)S(1)}, bf16[144,1152]{1,0:T(8,128)(2,1)S(1)}, u32[]{:S(2)}, u32[]{:S(2)}) collective-permute-start(bf16[144,1152]{1,0:T(8,128)(2,1)S(1)} %get-tuple-element.43), channel_id=1, source_target_pairs={{0,65},{1,64},{2,67},{3,66},{4,69},{5,68},{6,71},{7,70},{8,72},{9,... | collective-permute-start | bytes 995336 | tf_op jit(solution)/shard_map/ppermute | solution.py:35
  7.3 2.6 %collective-permute-done.2 = bf16[144,1152]{1,0:T(8,128)(2,1)S(1)} collective-permute-done((bf16[144,1152]{1,0:T(8,128)(2,1)S(1)}, bf16[144,1152]{1,0:T(8,128)(2,1)S(1)}, u32[]{:S(2)}, u32[]{:S(2)}) %collective-permute-start.2) | collective-permute-done | bytes 331808 | tf_op jit(solution)/shard_map/ppermute | solution.py:35
  10.4 2.5 %collective-permute-start.7 = (bf16[288,1152]{1,0:T(8,128)(2,1)S(1)}, bf16[288,1152]{1,0:T(8,128)(2,1)S(1)}, u32[]{:S(2)}, u32[]{:S(2)}) collective-permute-start(bf16[288,1152]{1,0:T(8,128)(2,1)S(1)} %concatenate.24.far), channel_id=1, source_target_pairs={{0,48},{1,49},{2,50},{3,51},{4,52},{5,53},{6,54},{7,55},{8,14},{9,... | collective-permute-start | bytes 1990664 | tf_op jit(solution)/shard_map/ppermute | solution.py:35
  13.0 2.8 %collective-permute-done = bf16[144,1152]{1,0:T(8,128)(2,1)S(1)} collective-permute-done((bf16[144,1152]{1,0:T(8,128)(2,1)S(1)}, bf16[144,1152]{1,0:T(8,128)(2,1)S(1)}, u32[]{:S(2)}, u32[]{:S(2)}) %collective-permute-start) | collective-permute-done | bytes 331808 | tf_op jit(solution)/shard_map/ppermute | solution.py:35
  16.3 2.8 %collective-permute-start.6 = (bf16[288,1152]{1,0:T(8,128)(2,1)S(1)}, bf16[288,1152]{1,0:T(8,128)(2,1)S(1)}, u32[]{:S(2)}, u32[]{:S(2)}) collective-permute-start(bf16[288,1152]{1,0:T(8,128)(2,1)S(1)} %concatenate.22.near), channel_id=1, source_target_pairs={{0,6},{1,7},{2,0},{3,1},{4,2},{5,3},{6,4},{7,5},{8,56},{9,57},{10,... | collective-permute-start | bytes 1990664 | tf_op jit(solution)/shard_map/ppermute | solution.py:35
  19.1 3.0 %broadcast_select_fusion = (bf16[1152,1152]{1,0:T(8,128)(2,1)S(1)}, bf16[1152,1152]{1,0:T(8,128)(2,1)S(1)}) fusion(bf16[1152,1152]{1,0:T(8,128)(2,1)} %param.10, bf16[1152,1152]{1,0:T(8,128)(2,1)} %param.9, pred[]{:T(512)S(6)} %eq.5), kind=kLoop, calls=%fused_computation | loop fusion | flops 2654208 | bytes 10616833 | tf_op jit(solution)/shard_map/jit(_where)/select_n | solution.py:391
  24.3 4.4 %collective-permute-start.8 = (bf16[832,1152]{1,0:T(8,128)(2,1)S(1)}, bf16[832,1152]{1,0:T(8,128)(2,1)S(1)}, u32[]{:S(2)}, u32[]{:S(2)}) collective-permute-start(bf16[832,1152]{1,0:T(8,128)(2,1)S(1)} %get-tuple-element.17.refs_0_), channel_id=1, source_target_pairs={{0,8},{1,9},{2,10},{3,11},{4,12},{5,13},{6,14},{7,15},{8,0},{9,1},... | collective-permute-start | bytes 5750792 | tf_op jit(solution)/shard_map/ppermute | solution.py:35
  28.7 4.0 %collective-permute-done.6.near = bf16[288,1152]{1,0:T(8,128)(2,1)S(1)} collective-permute-done((bf16[288,1152]{1,0:T(8,128)(2,1)S(1)}, bf16[288,1152]{1,0:T(8,128)(2,1)S(1)}, u32[]{:S(2)}, u32[]{:S(2)}) %collective-permute-start.6) | collective-permute-done | bytes 663584 | tf_op jit(solution)/shard_map/ppermute | solution.py:35
  41.2 2.8 %collective-permute-start.3 = (bf16[288,1152]{1,0:T(8,128)(2,1)S(1)}, bf16[288,1152]{1,0:T(8,128)(2,1)S(1)}, u32[]{:S(2)}, u32[]{:S(2)}) collective-permute-start(bf16[288,1152]{1,0:T(8,128)(2,1)S(1)} %concatenate.24.far), channel_id=1, source_target_pairs={{0,32},{1,33},{2,34},{3,35},{4,36},{5,37},{6,38},{7,39},{8,12},{9,... | collective-permute-start | bytes 1990664 | tf_op jit(solution)/shard_map/ppermute | solution.py:35
  45.4 17.1 %early_pairs.1.early = f32[1536,1152]{1,0:T(8,128)} custom-call(f32[3]{0:T(128)S(1)} %pad_maximum_fusion.5.knob_ref, bf16[832,1152]{1,0:T(8,128)(2,1)S(1)} %get-tuple-element.17.refs_0_, bf16[832,1152]{1,0:T(8,128)(2,1)S(1)} %get-tuple-element.18.refs_1_, bf16[832,1152]{1,0:T(8,128)(2,1)S(1)} %get-tuple-element.19.refs_2_, ...), custom_call_target="tpu_custom_call" | custom-call | flops 10871635968 | bytes 14000000 | tf_op jit(solution)/shard_map/early_pairs/pallas_call | solution.py:195
  66.5 3.7 %collective-permute-done.11.refs_7_ = bf16[832,1152]{1,0:T(8,128)(2,1)} collective-permute-done((bf16[832,1152]{1,0:T(8,128)(2,1)S(1)}, bf16[832,1152]{1,0:T(8,128)(2,1)}, u32[]{:S(2)}, u32[]{:S(2)}) %collective-permute-start.11) | collective-permute-done | bytes 1916960 | tf_op jit(solution)/shard_map/ppermute | solution.py:35
  70.2 26.7 %late_pairs.1 = (f32[288,1152]{1,0:T(8,128)}, bf16[288,1152]{1,0:T(8,128)(2,1)}, bf16[288,1152]{1,0:T(8,128)(2,1)}, bf16[288,1152]{1,0:T(8,128)(2,1)}) custom-call(s32[1]{0:T(128)} %bitcast.at_ref, f32[3]{0:T(128)} %copy-done, f32[1536,1152]{1,0:T(8,128)} %early_pairs.1.early, bf16[832,1152]{1,0:T(8,128)(2,1)} %copy-done.1, bf16[832,1152]{1,0:T(8,128)(2,1)} %copy-done.5, ...), custom_call_target="tpu_custom_call" | custom-call | flops 13891534848 | bytes 25000000 | tf_op jit(solution)/shard_map/late_pairs/pallas_call | solution.py:294
  100.5 14.8 %collective-permute-done.12 = bf16[288,1152]{1,0:T(8,128)(2,1)S(1)} collective-permute-done((bf16[288,1152]{1,0:T(8,128)(2,1)}, bf16[288,1152]{1,0:T(8,128)(2,1)S(1)}, u32[]{:S(2)}, u32[]{:S(2)}) %collective-permute-start.12) | collective-permute-done | bytes 663584 | tf_op jit(solution)/shard_map/ppermute | solution.py:35
  117.5 2.5 %collective-permute-start.16 = (f32[72,1152]{1,0:T(8,128)S(1)}, f32[72,1152]{1,0:T(8,128)S(1)}, u32[]{:S(2)}, u32[]{:S(2)}) collective-permute-start(f32[72,1152]{1,0:T(8,128)S(1)} %get-tuple-element.40), channel_id=1, source_target_pairs={{0,48},{1,49},{2,50},{3,51},{4,52},{5,53},{6,54},{7,55},{8,14},{9,... | collective-permute-start | bytes 995336 | tf_op jit(solution)/shard_map/ppermute | solution.py:35
  120.0 8.5 %collective-permute-done.15 = f32[72,1152]{1,0:T(8,128)S(1)} collective-permute-done((f32[72,1152]{1,0:T(8,128)S(1)}, f32[72,1152]{1,0:T(8,128)S(1)}, u32[]{:S(2)}, u32[]{:S(2)}) %collective-permute-start.15) | collective-permute-done | bytes 331808 | tf_op jit(solution)/shard_map/ppermute | solution.py:35
  131.3 2.6 %collective-permute-start.19 = (f32[72,1152]{1,0:T(8,128)S(1)}, f32[72,1152]{1,0:T(8,128)S(1)}, u32[]{:S(2)}, u32[]{:S(2)}) collective-permute-start(f32[72,1152]{1,0:T(8,128)S(1)} %get-tuple-element.35), channel_id=1, source_target_pairs={{0,65},{1,64},{2,67},{3,66},{4,69},{5,68},{6,71},{7,70},{8,73},{9,... | collective-permute-start | bytes 995336 | tf_op jit(solution)/shard_map/ppermute | solution.py:35
  134.7 5.8 %collective-permute-done.18 = f32[72,1152]{1,0:T(8,128)S(1)} collective-permute-done((f32[72,1152]{1,0:T(8,128)S(1)}, f32[72,1152]{1,0:T(8,128)S(1)}, u32[]{:S(2)}, u32[]{:S(2)}) %collective-permute-start.18) | collective-permute-done | bytes 331808 | tf_op jit(solution)/shard_map/ppermute | solution.py:35
  140.6 6.9 %collective-permute-done.20 = f32[72,1152]{1,0:T(8,128)S(1)} collective-permute-done((f32[72,1152]{1,0:T(8,128)S(1)}, f32[72,1152]{1,0:T(8,128)S(1)}, u32[]{:S(2)}, u32[]{:S(2)}) %collective-permute-start.20) | collective-permute-done | bytes 331808 | tf_op jit(solution)/shard_map/ppermute | solution.py:35
  153.5 3.0 %collective-permute-done.23 = bf16[72,1152]{1,0:T(8,128)(2,1)S(1)} collective-permute-done((bf16[72,1152]{1,0:T(8,128)(2,1)S(1)}, bf16[72,1152]{1,0:T(8,128)(2,1)S(1)}, u32[]{:S(2)}, u32[]{:S(2)}) %collective-permute-start.23) | collective-permute-done | bytes 165920 | tf_op jit(solution)/shard_map/ppermute | solution.py:35
  156.6 2.8 %collective-permute-start.25 = (bf16[288,1152]{1,0:T(8,128)(2,1)S(1)}, bf16[288,1152]{1,0:T(8,128)(2,1)S(1)}, u32[]{:S(2)}, u32[]{:S(2)}) collective-permute-start(bf16[288,1152]{1,0:T(8,128)(2,1)S(1)} %constant_dynamic-update-slice_fusion.refs_0_), channel_id=1, source_target_pairs={{0,6},{1,7},{2,0},{3,1},{4,2},{5,3},{6,4},{7,5},{8,56},{9,57},{10,... | collective-permute-start | bytes 1990664 | tf_op jit(solution)/shard_map/ppermute | solution.py:35
  160.5 4.8 %collective-permute-start.27 = (bf16[288,1152]{1,0:T(8,128)(2,1)S(1)}, bf16[288,1152]{1,0:T(8,128)(2,1)S(1)}, u32[]{:S(2)}, u32[]{:S(2)}) collective-permute-start(bf16[288,1152]{1,0:T(8,128)(2,1)S(1)} %constant_dynamic-update-slice_fusion.refs_0_), channel_id=1, source_target_pairs={{0,8},{1,9},{2,10},{3,11},{4,12},{5,13},{6,14},{7,15},{8,0},{9,1},... | collective-permute-start | bytes 1990664 | tf_op jit(solution)/shard_map/ppermute | solution.py:35
  167.7 5.2 %collective-permute-start.28 = (bf16[288,1152]{1,0:T(8,128)(2,1)S(1)}, bf16[288,1152]{1,0:T(8,128)(2,1)S(1)}, u32[]{:S(2)}, u32[]{:S(2)}) collective-permute-start(bf16[288,1152]{1,0:T(8,128)(2,1)S(1)} %collective-permute-done.24.refs_1_), channel_id=1, source_target_pairs={{0,8},{1,9},{2,10},{3,11},{4,12},{5,13},{6,14},{7,15},{8,0},{9,1},... | collective-permute-start | bytes 1990664 | tf_op jit(solution)/shard_map/ppermute | solution.py:35
  174.1 5.4 %collective-permute-start.29 = (bf16[288,1152]{1,0:T(8,128)(2,1)S(1)}, bf16[288,1152]{1,0:T(8,128)(2,1)S(1)}, u32[]{:S(2)}, u32[]{:S(2)}) collective-permute-start(bf16[288,1152]{1,0:T(8,128)(2,1)S(1)} %collective-permute-done.25.refs_2_), channel_id=1, source_target_pairs={{0,8},{1,9},{2,10},{3,11},{4,12},{5,13},{6,14},{7,15},{8,0},{9,1},... | collective-permute-start | bytes 1990664 | tf_op jit(solution)/shard_map/ppermute | solution.py:35
  182.8 4.2 %place.1 = (f32[1152,1152]{1,0:T(8,128)}, f32[1152,1152]{1,0:T(8,128)}) custom-call(bf16[288,1152]{1,0:T(8,128)(2,1)S(1)} %constant_dynamic-update-slice_fusion.refs_0_, bf16[288,1152]{1,0:T(8,128)(2,1)S(1)} %collective-permute-done.24.refs_1_, bf16[288,1152]{1,0:T(8,128)(2,1)S(1)} %collective-permute-done.25.refs_2_, ...), custom_call_target="tpu_custom_call" | custom-call | tf_op jit(solution)/shard_map/place/pallas_call | solution.py:352
  (100 shorter events, 43.2 us)
Async XLA Ops:
  2.5 7.3 %collective-permute-start.2 = (bf16[144,1152]{1,0:T(8,128)(2,1)S(1)}, bf16[144,1152]{1,0:T(8,128)(2,1)S(1)}, u32[]{:S(2)}, u32[]{:S(2)}) collective-permute-start(bf16[144,1152]{1,0:T(8,128)(2,1)S(1)} %get-tuple-element.43), channel_id=1, source_target_pairs={{0,65},{1,64},{2,67},{3,66},{4,69},{5,68},{6,71},{7,70},{8,72},{9,... | collective-permute-start | bytes 995336 | tf_op jit(solution)/shard_map/ppermute | solution.py:35
  5.1 10.7 %collective-permute-start = (bf16[144,1152]{1,0:T(8,128)(2,1)S(1)}, bf16[144,1152]{1,0:T(8,128)(2,1)S(1)}, u32[]{:S(2)}, u32[]{:S(2)}) collective-permute-start(bf16[144,1152]{1,0:T(8,128)(2,1)S(1)} %get-tuple-element.44), channel_id=1, source_target_pairs={{0,64},{1,65},{2,66},{3,67},{4,68},{5,69},{6,70},{7,71},{8,73},{9,... | collective-permute-start | bytes 995336 | tf_op jit(solution)/shard_map/ppermute | solution.py:35
  10.4 18.3 %collective-permute-start.7 = (bf16[288,1152]{1,0:T(8,128)(2,1)S(1)}, bf16[288,1152]{1,0:T(8,128)(2,1)S(1)}, u32[]{:S(2)}, u32[]{:S(2)}) collective-permute-start(bf16[288,1152]{1,0:T(8,128)(2,1)S(1)} %concatenate.24.far), channel_id=1, source_target_pairs={{0,48},{1,49},{2,50},{3,51},{4,52},{5,53},{6,54},{7,55},{8,14},{9,... | collective-permute-start | bytes 1990664 | tf_op jit(solution)/shard_map/ppermute | solution.py:35
  13.0 23.5 %collective-permute-start.5 = (bf16[288,1152]{1,0:T(8,128)(2,1)S(1)}, bf16[288,1152]{1,0:T(8,128)(2,1)S(1)}, u32[]{:S(2)}, u32[]{:S(2)}) collective-permute-start(bf16[288,1152]{1,0:T(8,128)(2,1)S(1)} %concatenate.24.far), channel_id=1, source_target_pairs={{0,16},{1,17},{2,18},{3,19},{4,20},{5,21},{6,22},{7,23},{8,10},{9,... | collective-permute-start | bytes 1990664 | tf_op jit(solution)/shard_map/ppermute | solution.py:35
  16.3 16.3 %collective-permute-start.6 = (bf16[288,1152]{1,0:T(8,128)(2,1)S(1)}, bf16[288,1152]{1,0:T(8,128)(2,1)S(1)}, u32[]{:S(2)}, u32[]{:S(2)}) collective-permute-start(bf16[288,1152]{1,0:T(8,128)(2,1)S(1)} %concatenate.22.near), channel_id=1, source_target_pairs={{0,6},{1,7},{2,0},{3,1},{4,2},{5,3},{6,4},{7,5},{8,56},{9,57},{10,... | collective-permute-start | bytes 1990664 | tf_op jit(solution)/shard_map/ppermute | solution.py:35
  19.1 17.4 %collective-permute-start.4 = (bf16[288,1152]{1,0:T(8,128)(2,1)S(1)}, bf16[288,1152]{1,0:T(8,128)(2,1)S(1)}, u32[]{:S(2)}, u32[]{:S(2)}) collective-permute-start(bf16[288,1152]{1,0:T(8,128)(2,1)S(1)} %concatenate.22.near), channel_id=1, source_target_pairs={{0,2},{1,3},{2,4},{3,5},{4,6},{5,7},{6,0},{7,1},{8,24},{9,25},{10,... | collective-permute-start | bytes 1990664 | tf_op jit(solution)/shard_map/ppermute | solution.py:35
  24.3 21.0 %collective-permute-start.8 = (bf16[832,1152]{1,0:T(8,128)(2,1)S(1)}, bf16[832,1152]{1,0:T(8,128)(2,1)S(1)}, u32[]{:S(2)}, u32[]{:S(2)}) collective-permute-start(bf16[832,1152]{1,0:T(8,128)(2,1)S(1)} %get-tuple-element.17.refs_0_), channel_id=1, source_target_pairs={{0,8},{1,9},{2,10},{3,11},{4,12},{5,13},{6,14},{7,15},{8,0},{9,1},... | collective-permute-start | bytes 5750792 | tf_op jit(solution)/shard_map/ppermute | solution.py:35
  34.8 10.5 %collective-permute-start.10 = (bf16[832,1152]{1,0:T(8,128)(2,1)S(1)}, bf16[832,1152]{1,0:T(8,128)(2,1)S(1)}, u32[]{:S(2)}, u32[]{:S(2)}) collective-permute-start(bf16[832,1152]{1,0:T(8,128)(2,1)S(1)} %get-tuple-element.19.refs_2_), channel_id=1, source_target_pairs={{0,8},{1,9},{2,10},{3,11},{4,12},{5,13},{6,14},{7,15},{8,0},{9,1},... | collective-permute-start | bytes 5750792 | tf_op jit(solution)/shard_map/ppermute | solution.py:35
  41.2 21.3 %collective-permute-start.3 = (bf16[288,1152]{1,0:T(8,128)(2,1)S(1)}, bf16[288,1152]{1,0:T(8,128)(2,1)S(1)}, u32[]{:S(2)}, u32[]{:S(2)}) collective-permute-start(bf16[288,1152]{1,0:T(8,128)(2,1)S(1)} %concatenate.24.far), channel_id=1, source_target_pairs={{0,32},{1,33},{2,34},{3,35},{4,36},{5,37},{6,38},{7,39},{8,12},{9,... | collective-permute-start | bytes 1990664 | tf_op jit(solution)/shard_map/ppermute | solution.py:35
  44.0 18.6 %collective-permute-start.1 = (bf16[288,1152]{1,0:T(8,128)(2,1)S(1)}, bf16[288,1152]{1,0:T(8,128)(2,1)S(1)}, u32[]{:S(2)}, u32[]{:S(2)}) collective-permute-start(bf16[288,1152]{1,0:T(8,128)(2,1)S(1)} %concatenate.22.near), channel_id=1, source_target_pairs={{0,4},{1,5},{2,6},{3,7},{4,0},{5,1},{6,2},{7,3},{8,40},{9,41},{10,... | collective-permute-start | bytes 1990664 | tf_op jit(solution)/shard_map/ppermute | solution.py:35
  96.9 18.4 %collective-permute-start.12 = (bf16[288,1152]{1,0:T(8,128)(2,1)}, bf16[288,1152]{1,0:T(8,128)(2,1)S(1)}, u32[]{:S(2)}, u32[]{:S(2)}) collective-permute-start(bf16[288,1152]{1,0:T(8,128)(2,1)} %get-tuple-element.29), channel_id=1, source_target_pairs={{0,2},{1,3},{2,4},{3,5},{4,6},{5,7},{6,0},{7,1},{8,24},{9,25},{10,... | collective-permute-start | bytes 1990664 | tf_op jit(solution)/shard_map/ppermute | solution.py:35
  98.6 16.7 %collective-permute-start.13 = (bf16[288,1152]{1,0:T(8,128)(2,1)}, bf16[288,1152]{1,0:T(8,128)(2,1)S(1)}, u32[]{:S(2)}, u32[]{:S(2)}) collective-permute-start(bf16[288,1152]{1,0:T(8,128)(2,1)} %get-tuple-element.30), channel_id=1, source_target_pairs={{0,6},{1,7},{2,0},{3,1},{4,2},{5,3},{6,4},{7,5},{8,56},{9,57},{10,... | collective-permute-start | bytes 1990664 | tf_op jit(solution)/shard_map/ppermute | solution.py:35
  99.6 15.7 %collective-permute-start.14 = (bf16[288,1152]{1,0:T(8,128)(2,1)}, bf16[288,1152]{1,0:T(8,128)(2,1)S(1)}, u32[]{:S(2)}, u32[]{:S(2)}) collective-permute-start(bf16[288,1152]{1,0:T(8,128)(2,1)} %get-tuple-element.31), channel_id=1, source_target_pairs={{0,4},{1,5},{2,6},{3,7},{4,0},{5,1},{6,2},{7,3},{8,40},{9,41},{10,... | collective-permute-start | bytes 1990664 | tf_op jit(solution)/shard_map/ppermute | solution.py:35
  117.0 11.4 %collective-permute-start.15 = (f32[72,1152]{1,0:T(8,128)S(1)}, f32[72,1152]{1,0:T(8,128)S(1)}, u32[]{:S(2)}, u32[]{:S(2)}) collective-permute-start(f32[72,1152]{1,0:T(8,128)S(1)} %get-tuple-element.38), channel_id=1, source_target_pairs={{0,16},{1,17},{2,18},{3,19},{4,20},{5,21},{6,22},{7,23},{8,10},{9,... | collective-permute-start | bytes 995336 | tf_op jit(solution)/shard_map/ppermute | solution.py:35
  117.5 10.9 %collective-permute-start.16 = (f32[72,1152]{1,0:T(8,128)S(1)}, f32[72,1152]{1,0:T(8,128)S(1)}, u32[]{:S(2)}, u32[]{:S(2)}) collective-permute-start(f32[72,1152]{1,0:T(8,128)S(1)} %get-tuple-element.40), channel_id=1, source_target_pairs={{0,48},{1,49},{2,50},{3,51},{4,52},{5,53},{6,54},{7,55},{8,14},{9,... | collective-permute-start | bytes 995336 | tf_op jit(solution)/shard_map/ppermute | solution.py:35
  120.0 9.2 %collective-permute-start.17 = (f32[72,1152]{1,0:T(8,128)S(1)}, f32[72,1152]{1,0:T(8,128)}, u32[]{:S(2)}, u32[]{:S(2)}) collective-permute-start(f32[72,1152]{1,0:T(8,128)S(1)} %get-tuple-element.39), channel_id=1, source_target_pairs={{0,32},{1,33},{2,34},{3,35},{4,36},{5,37},{6,38},{7,39},{8,12},{9,... | collective-permute-start | bytes 995336 | tf_op jit(solution)/shard_map/ppermute | solution.py:35
  131.2 9.3 %collective-permute-start.18 = (f32[72,1152]{1,0:T(8,128)S(1)}, f32[72,1152]{1,0:T(8,128)S(1)}, u32[]{:S(2)}, u32[]{:S(2)}) collective-permute-start(f32[72,1152]{1,0:T(8,128)S(1)} %get-tuple-element.35), channel_id=1, source_target_pairs={{0,64},{1,65},{2,66},{3,67},{4,68},{5,69},{6,70},{7,71},{8,72},{9,... | collective-permute-start | bytes 995336 | tf_op jit(solution)/shard_map/ppermute | solution.py:35
  131.3 9.2 %collective-permute-start.19 = (f32[72,1152]{1,0:T(8,128)S(1)}, f32[72,1152]{1,0:T(8,128)S(1)}, u32[]{:S(2)}, u32[]{:S(2)}) collective-permute-start(f32[72,1152]{1,0:T(8,128)S(1)} %get-tuple-element.35), channel_id=1, source_target_pairs={{0,65},{1,64},{2,67},{3,66},{4,69},{5,68},{6,71},{7,70},{8,73},{9,... | collective-permute-start | bytes 995336 | tf_op jit(solution)/shard_map/ppermute | solution.py:35
  134.0 13.5 %collective-permute-start.20 = (f32[72,1152]{1,0:T(8,128)S(1)}, f32[72,1152]{1,0:T(8,128)S(1)}, u32[]{:S(2)}, u32[]{:S(2)}) collective-permute-start(f32[72,1152]{1,0:T(8,128)S(1)} %get-tuple-element.35), channel_id=1, source_target_pairs={{0,1},{1,0},{2,3},{3,2},{4,5},{5,4},{6,7},{7,6},{8,9},{9,8},{10,11... | collective-permute-start | bytes 995336 | tf_op jit(solution)/shard_map/ppermute | solution.py:35
  156.5 11.2 %collective-permute-start.24 = (bf16[288,1152]{1,0:T(8,128)(2,1)S(1)}, bf16[288,1152]{1,0:T(8,128)(2,1)S(1)}, u32[]{:S(2)}, u32[]{:S(2)}) collective-permute-start(bf16[288,1152]{1,0:T(8,128)(2,1)S(1)} %constant_dynamic-update-slice_fusion.refs_0_), channel_id=1, source_target_pairs={{0,2},{1,3},{2,4},{3,5},{4,6},{5,7},{6,0},{7,1},{8,24},{9,25},{10,... | collective-permute-start | bytes 1990664 | tf_op jit(solution)/shard_map/ppermute | solution.py:35
  156.6 17.5 %collective-permute-start.25 = (bf16[288,1152]{1,0:T(8,128)(2,1)S(1)}, bf16[288,1152]{1,0:T(8,128)(2,1)S(1)}, u32[]{:S(2)}, u32[]{:S(2)}) collective-permute-start(bf16[288,1152]{1,0:T(8,128)(2,1)S(1)} %constant_dynamic-update-slice_fusion.refs_0_), channel_id=1, source_target_pairs={{0,6},{1,7},{2,0},{3,1},{4,2},{5,3},{6,4},{7,5},{8,56},{9,57},{10,... | collective-permute-start | bytes 1990664 | tf_op jit(solution)/shard_map/ppermute | solution.py:35
  159.4 20.1 %collective-permute-start.26 = (bf16[288,1152]{1,0:T(8,128)(2,1)S(1)}, bf16[288,1152]{1,0:T(8,128)(2,1)S(1)}, u32[]{:S(2)}, u32[]{:S(2)}) collective-permute-start(bf16[288,1152]{1,0:T(8,128)(2,1)S(1)} %constant_dynamic-update-slice_fusion.refs_0_), channel_id=1, source_target_pairs={{0,4},{1,5},{2,6},{3,7},{4,0},{5,1},{6,2},{7,3},{8,40},{9,41},{10,... | collective-permute-start | bytes 1990664 | tf_op jit(solution)/shard_map/ppermute | solution.py:35
  160.5 20.6 %collective-permute-start.27 = (bf16[288,1152]{1,0:T(8,128)(2,1)S(1)}, bf16[288,1152]{1,0:T(8,128)(2,1)S(1)}, u32[]{:S(2)}, u32[]{:S(2)}) collective-permute-start(bf16[288,1152]{1,0:T(8,128)(2,1)S(1)} %constant_dynamic-update-slice_fusion.refs_0_), channel_id=1, source_target_pairs={{0,8},{1,9},{2,10},{3,11},{4,12},{5,13},{6,14},{7,15},{8,0},{9,1},... | collective-permute-start | bytes 1990664 | tf_op jit(solution)/shard_map/ppermute | solution.py:35
  167.7 13.4 %collective-permute-start.28 = (bf16[288,1152]{1,0:T(8,128)(2,1)S(1)}, bf16[288,1152]{1,0:T(8,128)(2,1)S(1)}, u32[]{:S(2)}, u32[]{:S(2)}) collective-permute-start(bf16[288,1152]{1,0:T(8,128)(2,1)S(1)} %collective-permute-done.24.refs_1_), channel_id=1, source_target_pairs={{0,8},{1,9},{2,10},{3,11},{4,12},{5,13},{6,14},{7,15},{8,0},{9,1},... | collective-permute-start | bytes 1990664 | tf_op jit(solution)/shard_map/ppermute | solution.py:35
  (21 other events, 212.1 us)

commit v3 on v2

--- a/solution.py
+++ b/solution.py
@@ -75,22 +75,22 @@
 
 def id_row(coded):
     coded = coded.astype(F32)
-    parts = [coded[i : i + 1, :128] * 64.0 + coded[i : i + 1, 128:256] for i in (0, 16)]
+    parts = [coded[i : i + 1, :128] * 64.0 + coded[i : i + 1, 128:256] for i in (0, 1)]
     return jnp.concatenate(parts, axis=1)
 
 
 def project_kernel(near, far, head_near, head_far, message, rows_near):
-    sides = ((near, head_near, rows_near, 0, 0), (far, head_far, message, 576, 288))
+    sides = ((near, head_near, rows_near, 0, 0), (far, head_far, message, 544, 272))
     for block, head, rows, at, to in sides:
         rows[at : at + 256, :] = block[:256, :]
         projected = jnp.dot(block[:256, :], head[...], preferred_element_type=F32)
         inverse = lax.rsqrt(jnp.sum(projected * projected, axis=1, keepdims=True) + 1e-06)
         message[to : to + 256, :] = (projected * inverse).astype(BF16)
-        message[to + 256 : to + 288, :] = block[256:288, :]
+        message[to + 256 : to + 272, :] = block[256:272, :]
         rest = jnp.sum(jnp.where(eye_256(), inverse, 0.0), axis=0, keepdims=True)
         lines = lax.broadcasted_iota(jnp.int32, (16, 256), 0)
         coded = block[256:272, :256].astype(F32)
-        for line in (1, 2, 3):
+        for line in (2, 3, 4):
             part = rest.astype(BF16).astype(F32)
             coded = jnp.where(lines == line, part, coded)
             rest = rest - part
@@ -102,7 +102,7 @@
     return pl.pallas_call(
         project_kernel,
         out_shape=[
-            jax.ShapeDtypeStruct((832, WIDE), BF16),
+            jax.ShapeDtypeStruct((800, WIDE), BF16),
             jax.ShapeDtypeStruct((256, WIDE), BF16),
         ],
         in_specs=[whole] * 4,
@@ -119,7 +119,7 @@
     loads = []
     for i, (source, start) in enumerate(sources):
         rows = source.at[pl.ds(start, 256), :]
-        coded = source.at[pl.ds(start + 256, 32), pl.ds(0, 256)]
+        coded = source.at[pl.ds(start + 256, 16), pl.ds(0, 256)]
         loads.append(
             (
                 pltpu.make_async_copy(rows, units.at[pl.ds(i * 256, 256), :], unit_sems.at[i]),
@@ -151,15 +151,15 @@
     parts = []
     for i in range(2):
         coded = ids[2 * step + i].astype(F32)
-        parts.append(as_column(coded[1:2] + coded[2:3] + coded[3:4]))
+        parts.append(as_column(coded[2:3] + coded[3:4] + coded[4:5]))
     return jnp.concatenate(parts, axis=0)
 
 
 def unit_sources(own, over):
     near, far = [], []
     for mine, theirs in zip(own, over):
-        near += [(mine, 0), (theirs, 288)]
-        far += [(mine, 288), (theirs, 0)]
+        near += [(mine, 0), (theirs, 272)]
+        far += [(mine, 272), (theirs, 0)]
     return near, far
 
 
@@ -201,9 +201,9 @@
         out_specs=pl.BlockSpec((512, WIDE), lambda i: (i, 0)),
         scratch_shapes=[
             pltpu.VMEM((1536, WIDE), BF16),
-            pltpu.VMEM((6, 32, 256), BF16),
+            pltpu.VMEM((6, 16, 256), BF16),
             pltpu.VMEM((1536, WIDE), BF16),
-            pltpu.VMEM((6, 32, 256), BF16),
+            pltpu.VMEM((6, 16, 256), BF16),
             pltpu.VMEM((512, 1536), BF16),
             pltpu.SemaphoreType.DMA((4, 6)),
         ],
@@ -225,7 +225,7 @@
     near_loads = unit_loads(near_sources, near, near_ids, sems.at[0], sems.at[1])
     far_loads = unit_loads(far_sources, far, far_ids, sems.at[2], sems.at[3])
     for i in range(8):
-        source = over[i // 2].at[pl.ds(576, 256), :] if i % 2 else own_rows[i // 2]
+        source = over[i // 2].at[pl.ds(544, 256), :] if i % 2 else own_rows[i // 2]
         near_loads[i] += (
             pltpu.make_async_copy(source, rows.at[pl.ds(i * 256, 256), :], more_sems.at[0, i]),
         )
@@ -302,9 +302,9 @@
         * 4,
         scratch_shapes=[
             pltpu.VMEM((ROWS, WIDE), BF16),
-            pltpu.VMEM((8, 32, 256), BF16),
+            pltpu.VMEM((8, 16, 256), BF16),
             pltpu.VMEM((ROWS, WIDE), BF16),
-            pltpu.VMEM((8, 32, 256), BF16),
+            pltpu.VMEM((8, 16, 256), BF16),
             pltpu.VMEM((ROWS, WIDE), BF16),
             pltpu.VMEM((3, 512, WIDE), F32),
             pltpu.VMEM((512, ROWS), BF16),
@@ -392,7 +392,9 @@
 
     got = [send(mine, z_pair(0)), send(theirs, z_pair(1))]
     mine, theirs = [
-        jnp.concatenate([block[:128], other[:128], block[128:], other[128:]], axis=0)
+        jnp.concatenate(
+            [block[:128], other[:128], block[128:129], other[128:129], block[130:]], axis=0
+        )
         for block, other in zip((mine, theirs), got)
     ]
     blocks = [(mine, theirs)]

time: 187 us -> 186 us (level)
  transfers between devices with their start and end apart: 31 -> 31, of which waited for: 14 -> 13; matrix products, arithmetic and copies ran while one was open for 2% -> 2% of each run, Pallas kernels for 12% -> 13%
where the time goes in v3:
time: 186 us
  waiting for transfers between devices  58.4 us (31%)
  starting transfers between devices  57.1 us (31%)
  Pallas kernels  56.3 us (30%)
  other arithmetic  7.82 us (4%)
  local copies, waits for them, and re-layouts  4.05 us (2%)
  between operations  2.55 us (1%)
    ppermute x31, waiting for transfers between devices, send(): return lax.ppermute(value, AXES, routes(move))  58.4 us
    ppermute x31, starting transfers between devices, send(): return lax.ppermute(value, AXES, routes(move))  57.1 us
    pallas_call x1, Pallas kernels, late_pairs(): pl.pallas_call(late_kernel, grid=(4,), out_shape=[jax.ShapeDtypeStruct((2...  26.7 us
    pallas_call x1, Pallas kernels, early_pairs(): pl.pallas_call(early_kernel, grid=(3,), out_shape=jax.ShapeDtypeStruct((1...  17.1 us
    pallas_call x4, Pallas kernels, project(): pl.pallas_call(project_kernel, out_shape=[jax.ShapeDtypeStruct((800, WIDE...  8.37 us
    pallas_call x1, Pallas kernels, place(): pl.pallas_call(place_kernel, out_shape=[jax.ShapeDtypeStruct((WIDE, WIDE)...  4.16 us
  transfers between devices with their start and end apart: 31, of which 13 were waited for; matrix products, arithmetic and copies ran while one was open for 2% of the time, Pallas kernels for 13%

profile of v3, /device:TPU:1, one launch (start us, length us, event | category | flops | bytes accessed | tf_op | source)
XLA Modules:
  0.0 186.2 jit_solution(13008682053848722342)
XLA Ops:
  2.7 2.5 %collective-permute-start.2 = (bf16[144,1152]{1,0:T(8,128)(2,1)S(1)}, bf16[144,1152]{1,0:T(8,128)(2,1)S(1)}, u32[]{:S(2)}, u32[]{:S(2)}) collective-permute-start(bf16[144,1152]{1,0:T(8,128)(2,1)S(1)} %get-tuple-element.43), channel_id=1, source_target_pairs={{0,65},{1,64},{2,67},{3,66},{4,69},{5,68},{6,71},{7,70},{8,72},{9,... | collective-permute-start | bytes 995336 | tf_op jit(solution)/shard_map/ppermute | solution.py:35
  7.5 2.6 %collective-permute-done.2 = bf16[144,1152]{1,0:T(8,128)(2,1)S(1)} collective-permute-done((bf16[144,1152]{1,0:T(8,128)(2,1)S(1)}, bf16[144,1152]{1,0:T(8,128)(2,1)S(1)}, u32[]{:S(2)}, u32[]{:S(2)}) %collective-permute-start.2) | collective-permute-done | bytes 331808 | tf_op jit(solution)/shard_map/ppermute | solution.py:35
  10.6 2.5 %collective-permute-start.7 = (bf16[272,1152]{1,0:T(8,128)(2,1)S(1)}, bf16[272,1152]{1,0:T(8,128)(2,1)S(1)}, u32[]{:S(2)}, u32[]{:S(2)}) collective-permute-start(bf16[272,1152]{1,0:T(8,128)(2,1)S(1)} %concatenate.22.far), channel_id=1, source_target_pairs={{0,48},{1,49},{2,50},{3,51},{4,52},{5,53},{6,54},{7,55},{8,14},{9,... | collective-permute-start | bytes 1880072 | tf_op jit(solution)/shard_map/ppermute | solution.py:35
  13.2 2.8 %collective-permute-done = bf16[144,1152]{1,0:T(8,128)(2,1)S(1)} collective-permute-done((bf16[144,1152]{1,0:T(8,128)(2,1)S(1)}, bf16[144,1152]{1,0:T(8,128)(2,1)S(1)}, u32[]{:S(2)}, u32[]{:S(2)}) %collective-permute-start) | collective-permute-done | bytes 331808 | tf_op jit(solution)/shard_map/ppermute | solution.py:35
  16.6 2.8 %collective-permute-start.6 = (bf16[272,1152]{1,0:T(8,128)(2,1)S(1)}, bf16[272,1152]{1,0:T(8,128)(2,1)S(1)}, u32[]{:S(2)}, u32[]{:S(2)}) collective-permute-start(bf16[272,1152]{1,0:T(8,128)(2,1)S(1)} %concatenate.20.near), channel_id=1, source_target_pairs={{0,6},{1,7},{2,0},{3,1},{4,2},{5,3},{6,4},{7,5},{8,56},{9,57},{10,... | collective-permute-start | bytes 1880072 | tf_op jit(solution)/shard_map/ppermute | solution.py:35
  19.4 3.0 %broadcast_select_fusion = (bf16[1152,1152]{1,0:T(8,128)(2,1)S(1)}, bf16[1152,1152]{1,0:T(8,128)(2,1)S(1)}) fusion(bf16[1152,1152]{1,0:T(8,128)(2,1)} %param.10, bf16[1152,1152]{1,0:T(8,128)(2,1)} %param.9, pred[]{:T(512)S(6)} %eq.5), kind=kLoop, calls=%fused_computation | loop fusion | flops 2654208 | bytes 10616833 | tf_op jit(solution)/shard_map/jit(_where)/select_n | solution.py:391
  24.5 4.5 %collective-permute-start.8 = (bf16[800,1152]{1,0:T(8,128)(2,1)S(1)}, bf16[800,1152]{1,0:T(8,128)(2,1)S(1)}, u32[]{:S(2)}, u32[]{:S(2)}) collective-permute-start(bf16[800,1152]{1,0:T(8,128)(2,1)S(1)} %get-tuple-element.17.refs_0_), channel_id=1, source_target_pairs={{0,8},{1,9},{2,10},{3,11},{4,12},{5,13},{6,14},{7,15},{8,0},{9,1},... | collective-permute-start | bytes 5529608 | tf_op jit(solution)/shard_map/ppermute | solution.py:35
  29.0 3.1 %collective-permute-done.6.near = bf16[272,1152]{1,0:T(8,128)(2,1)S(1)} collective-permute-done((bf16[272,1152]{1,0:T(8,128)(2,1)S(1)}, bf16[272,1152]{1,0:T(8,128)(2,1)S(1)}, u32[]{:S(2)}, u32[]{:S(2)}) %collective-permute-start.6) | collective-permute-done | bytes 626720 | tf_op jit(solution)/shard_map/ppermute | solution.py:35
  40.7 2.8 %collective-permute-start.3 = (bf16[272,1152]{1,0:T(8,128)(2,1)S(1)}, bf16[272,1152]{1,0:T(8,128)(2,1)S(1)}, u32[]{:S(2)}, u32[]{:S(2)}) collective-permute-start(bf16[272,1152]{1,0:T(8,128)(2,1)S(1)} %concatenate.22.far), channel_id=1, source_target_pairs={{0,32},{1,33},{2,34},{3,35},{4,36},{5,37},{6,38},{7,39},{8,12},{9,... | collective-permute-start | bytes 1880072 | tf_op jit(solution)/shard_map/ppermute | solution.py:35
  44.9 17.1 %early_pairs.1.early = f32[1536,1152]{1,0:T(8,128)} custom-call(f32[3]{0:T(128)S(1)} %pad_maximum_fusion.3.knob_ref, bf16[800,1152]{1,0:T(8,128)(2,1)S(1)} %get-tuple-element.17.refs_0_, bf16[800,1152]{1,0:T(8,128)(2,1)S(1)} %get-tuple-element.18.refs_1_, bf16[800,1152]{1,0:T(8,128)(2,1)S(1)} %get-tuple-element.19.refs_2_, ...), custom_call_target="tpu_custom_call" | custom-call | flops 10871635968 | bytes 14000000 | tf_op jit(solution)/shard_map/early_pairs/pallas_call | solution.py:195
  66.0 3.6 %collective-permute-done.11.refs_7_ = bf16[800,1152]{1,0:T(8,128)(2,1)} collective-permute-done((bf16[800,1152]{1,0:T(8,128)(2,1)S(1)}, bf16[800,1152]{1,0:T(8,128)(2,1)}, u32[]{:S(2)}, u32[]{:S(2)}) %collective-permute-start.11) | collective-permute-done | bytes 1843232 | tf_op jit(solution)/shard_map/ppermute | solution.py:35
  69.5 26.7 %late_pairs.1 = (f32[288,1152]{1,0:T(8,128)}, bf16[288,1152]{1,0:T(8,128)(2,1)}, bf16[288,1152]{1,0:T(8,128)(2,1)}, bf16[288,1152]{1,0:T(8,128)(2,1)}) custom-call(s32[1]{0:T(128)} %bitcast.at_ref, f32[3]{0:T(128)} %copy-done, f32[1536,1152]{1,0:T(8,128)} %early_pairs.1.early, bf16[800,1152]{1,0:T(8,128)(2,1)} %copy-done.1, bf16[800,1152]{1,0:T(8,128)(2,1)} %copy-done.5, ...), custom_call_target="tpu_custom_call" | custom-call | flops 13891534848 | bytes 25000000 | tf_op jit(solution)/shard_map/late_pairs/pallas_call | solution.py:294
  99.7 14.9 %collective-permute-done.12 = bf16[288,1152]{1,0:T(8,128)(2,1)S(1)} collective-permute-done((bf16[288,1152]{1,0:T(8,128)(2,1)}, bf16[288,1152]{1,0:T(8,128)(2,1)S(1)}, u32[]{:S(2)}, u32[]{:S(2)}) %collective-permute-start.12) | collective-permute-done | bytes 663584 | tf_op jit(solution)/shard_map/ppermute | solution.py:35
  119.1 8.5 %collective-permute-done.15 = f32[72,1152]{1,0:T(8,128)S(1)} collective-permute-done((f32[72,1152]{1,0:T(8,128)S(1)}, f32[72,1152]{1,0:T(8,128)S(1)}, u32[]{:S(2)}, u32[]{:S(2)}) %collective-permute-start.15) | collective-permute-done | bytes 331808 | tf_op jit(solution)/shard_map/ppermute | solution.py:35
  130.4 2.6 %collective-permute-start.19 = (f32[72,1152]{1,0:T(8,128)S(1)}, f32[72,1152]{1,0:T(8,128)S(1)}, u32[]{:S(2)}, u32[]{:S(2)}) collective-permute-start(f32[72,1152]{1,0:T(8,128)S(1)} %get-tuple-element.35), channel_id=1, source_target_pairs={{0,65},{1,64},{2,67},{3,66},{4,69},{5,68},{6,71},{7,70},{8,73},{9,... | collective-permute-start | bytes 995336 | tf_op jit(solution)/shard_map/ppermute | solution.py:35
  133.5 6.3 %collective-permute-done.18 = f32[72,1152]{1,0:T(8,128)S(1)} collective-permute-done((f32[72,1152]{1,0:T(8,128)S(1)}, f32[72,1152]{1,0:T(8,128)S(1)}, u32[]{:S(2)}, u32[]{:S(2)}) %collective-permute-start.18) | collective-permute-done | bytes 331808 | tf_op jit(solution)/shard_map/ppermute | solution.py:35
  139.9 6.4 %collective-permute-done.20 = f32[72,1152]{1,0:T(8,128)S(1)} collective-permute-done((f32[72,1152]{1,0:T(8,128)S(1)}, f32[72,1152]{1,0:T(8,128)S(1)}, u32[]{:S(2)}, u32[]{:S(2)}) %collective-permute-start.20) | collective-permute-done | bytes 331808 | tf_op jit(solution)/shard_map/ppermute | solution.py:35
  147.2 2.7 %collective-permute-start.22 = (bf16[72,1152]{1,0:T(8,128)(2,1)S(1)}, bf16[72,1152]{1,0:T(8,128)(2,1)S(1)}, u32[]{:S(2)}, u32[]{:S(2)}) collective-permute-start(bf16[72,1152]{1,0:T(8,128)(2,1)S(1)} %get-tuple-element.33), channel_id=1, source_target_pairs={{0,48},{1,49},{2,50},{3,51},{4,52},{5,53},{6,54},{7,55},{8,14},{9,... | collective-permute-start | bytes 497672 | tf_op jit(solution)/shard_map/ppermute | solution.py:35
  152.6 3.0 %collective-permute-done.23 = bf16[72,1152]{1,0:T(8,128)(2,1)S(1)} collective-permute-done((bf16[72,1152]{1,0:T(8,128)(2,1)S(1)}, bf16[72,1152]{1,0:T(8,128)(2,1)S(1)}, u32[]{:S(2)}, u32[]{:S(2)}) %collective-permute-start.23) | collective-permute-done | bytes 165920 | tf_op jit(solution)/shard_map/ppermute | solution.py:35
  155.7 2.8 %collective-permute-start.25 = (bf16[288,1152]{1,0:T(8,128)(2,1)S(1)}, bf16[288,1152]{1,0:T(8,128)(2,1)S(1)}, u32[]{:S(2)}, u32[]{:S(2)}) collective-permute-start(bf16[288,1152]{1,0:T(8,128)(2,1)S(1)} %constant_dynamic-update-slice_fusion.refs_0_), channel_id=1, source_target_pairs={{0,6},{1,7},{2,0},{3,1},{4,2},{5,3},{6,4},{7,5},{8,56},{9,57},{10,... | collective-permute-start | bytes 1990664 | tf_op jit(solution)/shard_map/ppermute | solution.py:35
  159.6 4.8 %collective-permute-start.27 = (bf16[288,1152]{1,0:T(8,128)(2,1)S(1)}, bf16[288,1152]{1,0:T(8,128)(2,1)S(1)}, u32[]{:S(2)}, u32[]{:S(2)}) collective-permute-start(bf16[288,1152]{1,0:T(8,128)(2,1)S(1)} %constant_dynamic-update-slice_fusion.refs_0_), channel_id=1, source_target_pairs={{0,8},{1,9},{2,10},{3,11},{4,12},{5,13},{6,14},{7,15},{8,0},{9,1},... | collective-permute-start | bytes 1990664 | tf_op jit(solution)/shard_map/ppermute | solution.py:35
  166.8 4.9 %collective-permute-start.28 = (bf16[288,1152]{1,0:T(8,128)(2,1)S(1)}, bf16[288,1152]{1,0:T(8,128)(2,1)S(1)}, u32[]{:S(2)}, u32[]{:S(2)}) collective-permute-start(bf16[288,1152]{1,0:T(8,128)(2,1)S(1)} %collective-permute-done.24.refs_1_), channel_id=1, source_target_pairs={{0,8},{1,9},{2,10},{3,11},{4,12},{5,13},{6,14},{7,15},{8,0},{9,1},... | collective-permute-start | bytes 1990664 | tf_op jit(solution)/shard_map/ppermute | solution.py:35
  173.2 5.1 %collective-permute-start.29 = (bf16[288,1152]{1,0:T(8,128)(2,1)S(1)}, bf16[288,1152]{1,0:T(8,128)(2,1)S(1)}, u32[]{:S(2)}, u32[]{:S(2)}) collective-permute-start(bf16[288,1152]{1,0:T(8,128)(2,1)S(1)} %collective-permute-done.25.refs_2_), channel_id=1, source_target_pairs={{0,8},{1,9},{2,10},{3,11},{4,12},{5,13},{6,14},{7,15},{8,0},{9,1},... | collective-permute-start | bytes 1990664 | tf_op jit(solution)/shard_map/ppermute | solution.py:35
  181.8 4.2 %place.1 = (f32[1152,1152]{1,0:T(8,128)}, f32[1152,1152]{1,0:T(8,128)}) custom-call(bf16[288,1152]{1,0:T(8,128)(2,1)S(1)} %constant_dynamic-update-slice_fusion.refs_0_, bf16[288,1152]{1,0:T(8,128)(2,1)S(1)} %collective-permute-done.24.refs_1_, bf16[288,1152]{1,0:T(8,128)(2,1)S(1)} %collective-permute-done.25.refs_2_, ...), custom_call_target="tpu_custom_call" | custom-call | tf_op jit(solution)/shard_map/place/pallas_call | solution.py:352
  (102 shorter events, 43.4 us)
Async XLA Ops:
  2.7 7.3 %collective-permute-start.2 = (bf16[144,1152]{1,0:T(8,128)(2,1)S(1)}, bf16[144,1152]{1,0:T(8,128)(2,1)S(1)}, u32[]{:S(2)}, u32[]{:S(2)}) collective-permute-start(bf16[144,1152]{1,0:T(8,128)(2,1)S(1)} %get-tuple-element.43), channel_id=1, source_target_pairs={{0,65},{1,64},{2,67},{3,66},{4,69},{5,68},{6,71},{7,70},{8,72},{9,... | collective-permute-start | bytes 995336 | tf_op jit(solution)/shard_map/ppermute | solution.py:35
  5.3 10.7 %collective-permute-start = (bf16[144,1152]{1,0:T(8,128)(2,1)S(1)}, bf16[144,1152]{1,0:T(8,128)(2,1)S(1)}, u32[]{:S(2)}, u32[]{:S(2)}) collective-permute-start(bf16[144,1152]{1,0:T(8,128)(2,1)S(1)} %get-tuple-element.44), channel_id=1, source_target_pairs={{0,64},{1,65},{2,66},{3,67},{4,68},{5,69},{6,70},{7,71},{8,73},{9,... | collective-permute-start | bytes 995336 | tf_op jit(solution)/shard_map/ppermute | solution.py:35
  10.6 18.3 %collective-permute-start.7 = (bf16[272,1152]{1,0:T(8,128)(2,1)S(1)}, bf16[272,1152]{1,0:T(8,128)(2,1)S(1)}, u32[]{:S(2)}, u32[]{:S(2)}) collective-permute-start(bf16[272,1152]{1,0:T(8,128)(2,1)S(1)} %concatenate.22.far), channel_id=1, source_target_pairs={{0,48},{1,49},{2,50},{3,51},{4,52},{5,53},{6,54},{7,55},{8,14},{9,... | collective-permute-start | bytes 1880072 | tf_op jit(solution)/shard_map/ppermute | solution.py:35
  13.2 22.7 %collective-permute-start.5 = (bf16[272,1152]{1,0:T(8,128)(2,1)S(1)}, bf16[272,1152]{1,0:T(8,128)(2,1)S(1)}, u32[]{:S(2)}, u32[]{:S(2)}) collective-permute-start(bf16[272,1152]{1,0:T(8,128)(2,1)S(1)} %concatenate.22.far), channel_id=1, source_target_pairs={{0,16},{1,17},{2,18},{3,19},{4,20},{5,21},{6,22},{7,23},{8,10},{9,... | collective-permute-start | bytes 1880072 | tf_op jit(solution)/shard_map/ppermute | solution.py:35
  16.6 15.5 %collective-permute-start.6 = (bf16[272,1152]{1,0:T(8,128)(2,1)S(1)}, bf16[272,1152]{1,0:T(8,128)(2,1)S(1)}, u32[]{:S(2)}, u32[]{:S(2)}) collective-permute-start(bf16[272,1152]{1,0:T(8,128)(2,1)S(1)} %concatenate.20.near), channel_id=1, source_target_pairs={{0,6},{1,7},{2,0},{3,1},{4,2},{5,3},{6,4},{7,5},{8,56},{9,57},{10,... | collective-permute-start | bytes 1880072 | tf_op jit(solution)/shard_map/ppermute | solution.py:35
  19.4 16.6 %collective-permute-start.4 = (bf16[272,1152]{1,0:T(8,128)(2,1)S(1)}, bf16[272,1152]{1,0:T(8,128)(2,1)S(1)}, u32[]{:S(2)}, u32[]{:S(2)}) collective-permute-start(bf16[272,1152]{1,0:T(8,128)(2,1)S(1)} %concatenate.20.near), channel_id=1, source_target_pairs={{0,2},{1,3},{2,4},{3,5},{4,6},{5,7},{6,0},{7,1},{8,24},{9,25},{10,... | collective-permute-start | bytes 1880072 | tf_op jit(solution)/shard_map/ppermute | solution.py:35
  24.5 20.3 %collective-permute-start.8 = (bf16[800,1152]{1,0:T(8,128)(2,1)S(1)}, bf16[800,1152]{1,0:T(8,128)(2,1)S(1)}, u32[]{:S(2)}, u32[]{:S(2)}) collective-permute-start(bf16[800,1152]{1,0:T(8,128)(2,1)S(1)} %get-tuple-element.17.refs_0_), channel_id=1, source_target_pairs={{0,8},{1,9},{2,10},{3,11},{4,12},{5,13},{6,14},{7,15},{8,0},{9,1},... | collective-permute-start | bytes 5529608 | tf_op jit(solution)/shard_map/ppermute | solution.py:35
  34.2 10.6 %collective-permute-start.10 = (bf16[800,1152]{1,0:T(8,128)(2,1)S(1)}, bf16[800,1152]{1,0:T(8,128)(2,1)S(1)}, u32[]{:S(2)}, u32[]{:S(2)}) collective-permute-start(bf16[800,1152]{1,0:T(8,128)(2,1)S(1)} %get-tuple-element.19.refs_2_), channel_id=1, source_target_pairs={{0,8},{1,9},{2,10},{3,11},{4,12},{5,13},{6,14},{7,15},{8,0},{9,1},... | collective-permute-start | bytes 5529608 | tf_op jit(solution)/shard_map/ppermute | solution.py:35
  40.7 21.3 %collective-permute-start.3 = (bf16[272,1152]{1,0:T(8,128)(2,1)S(1)}, bf16[272,1152]{1,0:T(8,128)(2,1)S(1)}, u32[]{:S(2)}, u32[]{:S(2)}) collective-permute-start(bf16[272,1152]{1,0:T(8,128)(2,1)S(1)} %concatenate.22.far), channel_id=1, source_target_pairs={{0,32},{1,33},{2,34},{3,35},{4,36},{5,37},{6,38},{7,39},{8,12},{9,... | collective-permute-start | bytes 1880072 | tf_op jit(solution)/shard_map/ppermute | solution.py:35
  43.5 18.5 %collective-permute-start.1 = (bf16[272,1152]{1,0:T(8,128)(2,1)S(1)}, bf16[272,1152]{1,0:T(8,128)(2,1)S(1)}, u32[]{:S(2)}, u32[]{:S(2)}) collective-permute-start(bf16[272,1152]{1,0:T(8,128)(2,1)S(1)} %concatenate.20.near), channel_id=1, source_target_pairs={{0,4},{1,5},{2,6},{3,7},{4,0},{5,1},{6,2},{7,3},{8,40},{9,41},{10,... | collective-permute-start | bytes 1880072 | tf_op jit(solution)/shard_map/ppermute | solution.py:35
  96.2 18.4 %collective-permute-start.12 = (bf16[288,1152]{1,0:T(8,128)(2,1)}, bf16[288,1152]{1,0:T(8,128)(2,1)S(1)}, u32[]{:S(2)}, u32[]{:S(2)}) collective-permute-start(bf16[288,1152]{1,0:T(8,128)(2,1)} %get-tuple-element.29), channel_id=1, source_target_pairs={{0,2},{1,3},{2,4},{3,5},{4,6},{5,7},{6,0},{7,1},{8,24},{9,25},{10,... | collective-permute-start | bytes 1990664 | tf_op jit(solution)/shard_map/ppermute | solution.py:35
  97.9 16.8 %collective-permute-start.13 = (bf16[288,1152]{1,0:T(8,128)(2,1)}, bf16[288,1152]{1,0:T(8,128)(2,1)S(1)}, u32[]{:S(2)}, u32[]{:S(2)}) collective-permute-start(bf16[288,1152]{1,0:T(8,128)(2,1)} %get-tuple-element.30), channel_id=1, source_target_pairs={{0,6},{1,7},{2,0},{3,1},{4,2},{5,3},{6,4},{7,5},{8,56},{9,57},{10,... | collective-permute-start | bytes 1990664 | tf_op jit(solution)/shard_map/ppermute | solution.py:35
  99.0 15.7 %collective-permute-start.14 = (bf16[288,1152]{1,0:T(8,128)(2,1)}, bf16[288,1152]{1,0:T(8,128)(2,1)S(1)}, u32[]{:S(2)}, u32[]{:S(2)}) collective-permute-start(bf16[288,1152]{1,0:T(8,128)(2,1)} %get-tuple-element.31), channel_id=1, source_target_pairs={{0,4},{1,5},{2,6},{3,7},{4,0},{5,1},{6,2},{7,3},{8,40},{9,41},{10,... | collective-permute-start | bytes 1990664 | tf_op jit(solution)/shard_map/ppermute | solution.py:35
  116.4 11.2 %collective-permute-start.15 = (f32[72,1152]{1,0:T(8,128)S(1)}, f32[72,1152]{1,0:T(8,128)S(1)}, u32[]{:S(2)}, u32[]{:S(2)}) collective-permute-start(f32[72,1152]{1,0:T(8,128)S(1)} %get-tuple-element.38), channel_id=1, source_target_pairs={{0,16},{1,17},{2,18},{3,19},{4,20},{5,21},{6,22},{7,23},{8,10},{9,... | collective-permute-start | bytes 995336 | tf_op jit(solution)/shard_map/ppermute | solution.py:35
  116.6 11.0 %collective-permute-start.16 = (f32[72,1152]{1,0:T(8,128)S(1)}, f32[72,1152]{1,0:T(8,128)S(1)}, u32[]{:S(2)}, u32[]{:S(2)}) collective-permute-start(f32[72,1152]{1,0:T(8,128)S(1)} %get-tuple-element.40), channel_id=1, source_target_pairs={{0,48},{1,49},{2,50},{3,51},{4,52},{5,53},{6,54},{7,55},{8,14},{9,... | collective-permute-start | bytes 995336 | tf_op jit(solution)/shard_map/ppermute | solution.py:35
  119.1 9.2 %collective-permute-start.17 = (f32[72,1152]{1,0:T(8,128)S(1)}, f32[72,1152]{1,0:T(8,128)}, u32[]{:S(2)}, u32[]{:S(2)}) collective-permute-start(f32[72,1152]{1,0:T(8,128)S(1)} %get-tuple-element.39), channel_id=1, source_target_pairs={{0,32},{1,33},{2,34},{3,35},{4,36},{5,37},{6,38},{7,39},{8,12},{9,... | collective-permute-start | bytes 995336 | tf_op jit(solution)/shard_map/ppermute | solution.py:35
  130.3 9.5 %collective-permute-start.18 = (f32[72,1152]{1,0:T(8,128)S(1)}, f32[72,1152]{1,0:T(8,128)S(1)}, u32[]{:S(2)}, u32[]{:S(2)}) collective-permute-start(f32[72,1152]{1,0:T(8,128)S(1)} %get-tuple-element.35), channel_id=1, source_target_pairs={{0,64},{1,65},{2,66},{3,67},{4,68},{5,69},{6,70},{7,71},{8,72},{9,... | collective-permute-start | bytes 995336 | tf_op jit(solution)/shard_map/ppermute | solution.py:35
  130.4 9.4 %collective-permute-start.19 = (f32[72,1152]{1,0:T(8,128)S(1)}, f32[72,1152]{1,0:T(8,128)S(1)}, u32[]{:S(2)}, u32[]{:S(2)}) collective-permute-start(f32[72,1152]{1,0:T(8,128)S(1)} %get-tuple-element.35), channel_id=1, source_target_pairs={{0,65},{1,64},{2,67},{3,66},{4,69},{5,68},{6,71},{7,70},{8,73},{9,... | collective-permute-start | bytes 995336 | tf_op jit(solution)/shard_map/ppermute | solution.py:35
  133.1 13.3 %collective-permute-start.20 = (f32[72,1152]{1,0:T(8,128)S(1)}, f32[72,1152]{1,0:T(8,128)S(1)}, u32[]{:S(2)}, u32[]{:S(2)}) collective-permute-start(f32[72,1152]{1,0:T(8,128)S(1)} %get-tuple-element.35), channel_id=1, source_target_pairs={{0,1},{1,0},{2,3},{3,2},{4,5},{5,4},{6,7},{7,6},{8,9},{9,8},{10,11... | collective-permute-start | bytes 995336 | tf_op jit(solution)/shard_map/ppermute | solution.py:35
  155.6 11.2 %collective-permute-start.24 = (bf16[288,1152]{1,0:T(8,128)(2,1)S(1)}, bf16[288,1152]{1,0:T(8,128)(2,1)S(1)}, u32[]{:S(2)}, u32[]{:S(2)}) collective-permute-start(bf16[288,1152]{1,0:T(8,128)(2,1)S(1)} %constant_dynamic-update-slice_fusion.refs_0_), channel_id=1, source_target_pairs={{0,2},{1,3},{2,4},{3,5},{4,6},{5,7},{6,0},{7,1},{8,24},{9,25},{10,... | collective-permute-start | bytes 1990664 | tf_op jit(solution)/shard_map/ppermute | solution.py:35
  155.7 17.5 %collective-permute-start.25 = (bf16[288,1152]{1,0:T(8,128)(2,1)S(1)}, bf16[288,1152]{1,0:T(8,128)(2,1)S(1)}, u32[]{:S(2)}, u32[]{:S(2)}) collective-permute-start(bf16[288,1152]{1,0:T(8,128)(2,1)S(1)} %constant_dynamic-update-slice_fusion.refs_0_), channel_id=1, source_target_pairs={{0,6},{1,7},{2,0},{3,1},{4,2},{5,3},{6,4},{7,5},{8,56},{9,57},{10,... | collective-permute-start | bytes 1990664 | tf_op jit(solution)/shard_map/ppermute | solution.py:35
  158.5 19.9 %collective-permute-start.26 = (bf16[288,1152]{1,0:T(8,128)(2,1)S(1)}, bf16[288,1152]{1,0:T(8,128)(2,1)S(1)}, u32[]{:S(2)}, u32[]{:S(2)}) collective-permute-start(bf16[288,1152]{1,0:T(8,128)(2,1)S(1)} %constant_dynamic-update-slice_fusion.refs_0_), channel_id=1, source_target_pairs={{0,4},{1,5},{2,6},{3,7},{4,0},{5,1},{6,2},{7,3},{8,40},{9,41},{10,... | collective-permute-start | bytes 1990664 | tf_op jit(solution)/shard_map/ppermute | solution.py:35
  159.6 20.5 %collective-permute-start.27 = (bf16[288,1152]{1,0:T(8,128)(2,1)S(1)}, bf16[288,1152]{1,0:T(8,128)(2,1)S(1)}, u32[]{:S(2)}, u32[]{:S(2)}) collective-permute-start(bf16[288,1152]{1,0:T(8,128)(2,1)S(1)} %constant_dynamic-update-slice_fusion.refs_0_), channel_id=1, source_target_pairs={{0,8},{1,9},{2,10},{3,11},{4,12},{5,13},{6,14},{7,15},{8,0},{9,1},... | collective-permute-start | bytes 1990664 | tf_op jit(solution)/shard_map/ppermute | solution.py:35
  166.8 13.3 %collective-permute-start.28 = (bf16[288,1152]{1,0:T(8,128)(2,1)S(1)}, bf16[288,1152]{1,0:T(8,128)(2,1)S(1)}, u32[]{:S(2)}, u32[]{:S(2)}) collective-permute-start(bf16[288,1152]{1,0:T(8,128)(2,1)S(1)} %collective-permute-done.24.refs_1_), channel_id=1, source_target_pairs={{0,8},{1,9},{2,10},{3,11},{4,12},{5,13},{6,14},{7,15},{8,0},{9,1},... | collective-permute-start | bytes 1990664 | tf_op jit(solution)/shard_map/ppermute | solution.py:35
  (21 other events, 211.0 us)

commit v4 on v3

--- a/solution.py
+++ b/solution.py
@@ -82,7 +82,8 @@
 def project_kernel(near, far, head_near, head_far, message, rows_near):
     sides = ((near, head_near, rows_near, 0, 0), (far, head_far, message, 544, 272))
     for block, head, rows, at, to in sides:
-        rows[at : at + 256, :] = block[:256, :]
+        if rows.shape[0] > at:
+            rows[at : at + 256, :] = block[:256, :]
         projected = jnp.dot(block[:256, :], head[...], preferred_element_type=F32)
         inverse = lax.rsqrt(jnp.sum(projected * projected, axis=1, keepdims=True) + 1e-06)
         message[to : to + 256, :] = (projected * inverse).astype(BF16)
@@ -97,12 +98,12 @@
         message[to + 256 : to + 272, :256] = coded.astype(BF16)
 
 
-def project(near, far, heads):
+def project(near, far, heads, message_rows):
     whole = pl.BlockSpec(memory_space=pltpu.VMEM)
     return pl.pallas_call(
         project_kernel,
         out_shape=[
-            jax.ShapeDtypeStruct((800, WIDE), BF16),
+            jax.ShapeDtypeStruct((message_rows, WIDE), BF16),
             jax.ShapeDtypeStruct((256, WIDE), BF16),
         ],
         in_specs=[whole] * 4,
@@ -218,14 +219,16 @@
 
 
 def late_kernel(at_ref, knob_ref, early, *refs):
-    own, over, own_rows, outs = refs[:4], refs[4:8], refs[8:12], refs[12:16]
-    near, near_ids, far, far_ids, rows, grad, coef, total, sems, more_sems = refs[16:]
+    own, over, own_rows, outs = refs[:4], refs[4:8], refs[8:12], refs[13:17]
+    over_rows = [block.at[pl.ds(544, 256), :] for block in over[:3]]
+    over_rows.append(refs[12].at[pl.ds(0, 256), :])
+    near, near_ids, far, far_ids, rows, grad, coef, total, sems, more_sems = refs[17:]
     near_sources, far_sources = unit_sources(own, over)
     step = pl.program_id(0)
     near_loads = unit_loads(near_sources, near, near_ids, sems.at[0], sems.at[1])
     far_loads = unit_loads(far_sources, far, far_ids, sems.at[2], sems.at[3])
     for i in range(8):
-        source = over[i // 2].at[pl.ds(544, 256), :] if i % 2 else own_rows[i // 2]
+        source = over_rows[i // 2] if i % 2 else own_rows[i // 2]
         near_loads[i] += (
             pltpu.make_async_copy(source, rows.at[pl.ds(i * 256, 256), :], more_sems.at[0, i]),
         )
@@ -289,13 +292,13 @@
             out[...] = total[pl.ds(place, 288), :].astype(out.dtype)
 
 
-def late_pairs(at, knobs, early, own, over, own_rows):
+def late_pairs(at, knobs, early, own, over, own_rows, last_rows):
     smem = pl.BlockSpec(memory_space=pltpu.SMEM)
     return pl.pallas_call(
         late_kernel,
         grid=(4,),
         out_shape=[jax.ShapeDtypeStruct((288, WIDE), kind) for kind in (F32, BF16, BF16, BF16)],
-        in_specs=[smem, smem] + [pl.BlockSpec(memory_space=pl.ANY)] * 13,
+        in_specs=[smem, smem] + [pl.BlockSpec(memory_space=pl.ANY)] * 14,
         out_specs=[
             pl.BlockSpec((288, WIDE), lambda i: (0, 0), pipeline_mode=pl.Buffered(1))
         ]
@@ -321,7 +324,7 @@
             transcendentals=7 * 512 * 512,
         ),
         name="late_pairs",
-    )(at, knobs, early, *own, *over, *own_rows)
+    )(at, knobs, early, *own, *over, *own_rows, last_rows)
 
 
 def place_kernel(*refs):
@@ -403,7 +406,7 @@
     own, over, own_rows = [], [], []
 
     def take(turn):
-        message, rows = project(*blocks[turn], heads)
+        message, rows = project(*blocks[turn], heads, 800 if turn < 3 else 544)
         own.append(message)
         over.append(send(message, other_core))
         own_rows.append(rows)
@@ -412,13 +415,14 @@
         take(turn)
     early = early_pairs(knobs, own, over)
     blocks[3], early = lax.optimization_barrier((blocks[3], early))
+    last_rows = send(blocks[3][1], other_core)
     take(3)
 
     at_x = lax.axis_index("x")
     at_y = lax.axis_index("y")
     at_first = jnp.where(first, at_x, at_y)
     at_second = jnp.where(first, at_y, at_x)
-    part, *away = late_pairs(at_first[None], knobs, early, own, over, own_rows)
+    part, *away = late_pairs(at_first[None], knobs, early, own, over, own_rows, last_rows)
     part = added(part, [send(piece, ring(by, 0)) for by, piece in zip((1, 3, 2), away)])
     part = scattered(part, lambda by: ring(by, 1), at_second)
     moved = [send(part, z_ring(by)) for by in (1, 3, 2)]

time: 186 us -> 187 us (level)
    ppermute x31 -> x32, waiting for transfers between devices: 58.4 us -> 58.2 us  [send(): return lax.ppermute(value, AXES, routes(move))]
    ppermute x31 -> x32, starting transfers between devices: 57.1 us -> 57.2 us  [send(): return lax.ppermute(value, AXES, routes(move))]
  transfers between devices with their start and end apart: 31 -> 32, of which waited for: 13 -> 14; matrix products, arithmetic and copies ran while one was open for 2% -> 2% of each run, Pallas kernels for 13% -> 12%
where the time goes in v4:
time: 187 us
  waiting for transfers between devices  58.2 us (31%)
  starting transfers between devices  57.2 us (31%)
  Pallas kernels  56.3 us (30%)
  other arithmetic  7.82 us (4%)
  local copies, waits for them, and re-layouts  5.11 us (3%)
  between operations  2.55 us (1%)
    ppermute x32, waiting for transfers between devices, send(): return lax.ppermute(value, AXES, routes(move))  58.2 us
    ppermute x32, starting transfers between devices, send(): return lax.ppermute(value, AXES, routes(move))  57.2 us
    pallas_call x1, Pallas kernels, late_pairs(): pl.pallas_call(late_kernel, grid=(4,), out_shape=[jax.ShapeDtypeStruct((2...  26.7 us
    pallas_call x1, Pallas kernels, early_pairs(): pl.pallas_call(early_kernel, grid=(3,), out_shape=jax.ShapeDtypeStruct((1...  17.1 us
    pallas_call x4, Pallas kernels, project(): pl.pallas_call(project_kernel, out_shape=[jax.ShapeDtypeStruct((message_r...  8.29 us
    pallas_call x1, Pallas kernels, place(): pl.pallas_call(place_kernel, out_shape=[jax.ShapeDtypeStruct((WIDE, WIDE)...  4.16 us
  transfers between devices with their start and end apart: 32, of which 14 were waited for; matrix products, arithmetic and copies ran while one was open for 2% of the time, Pallas kernels for 12%

profile of v4, /device:TPU:1, one launch (start us, length us, event | category | flops | bytes accessed | tf_op | source)
XLA Modules:
  0.0 187.2 jit_solution(13432144458619406102)
XLA Ops:
  2.7 2.5 %collective-permute-start.2 = (bf16[144,1152]{1,0:T(8,128)(2,1)S(1)}, bf16[144,1152]{1,0:T(8,128)(2,1)S(1)}, u32[]{:S(2)}, u32[]{:S(2)}) collective-permute-start(bf16[144,1152]{1,0:T(8,128)(2,1)S(1)} %get-tuple-element.43), channel_id=1, source_target_pairs={{0,65},{1,64},{2,67},{3,66},{4,69},{5,68},{6,71},{7,70},{8,72},{9,... | collective-permute-start | bytes 995336 | tf_op jit(solution)/shard_map/ppermute | solution.py:35
  7.5 2.6 %collective-permute-done.2 = bf16[144,1152]{1,0:T(8,128)(2,1)S(1)} collective-permute-done((bf16[144,1152]{1,0:T(8,128)(2,1)S(1)}, bf16[144,1152]{1,0:T(8,128)(2,1)S(1)}, u32[]{:S(2)}, u32[]{:S(2)}) %collective-permute-start.2) | collective-permute-done | bytes 331808 | tf_op jit(solution)/shard_map/ppermute | solution.py:35
  10.6 2.5 %collective-permute-start.7 = (bf16[272,1152]{1,0:T(8,128)(2,1)S(1)}, bf16[272,1152]{1,0:T(8,128)(2,1)S(1)}, u32[]{:S(2)}, u32[]{:S(2)}) collective-permute-start(bf16[272,1152]{1,0:T(8,128)(2,1)S(1)} %concatenate.22.far), channel_id=1, source_target_pairs={{0,48},{1,49},{2,50},{3,51},{4,52},{5,53},{6,54},{7,55},{8,14},{9,... | collective-permute-start | bytes 1880072 | tf_op jit(solution)/shard_map/ppermute | solution.py:35
  13.2 2.8 %collective-permute-done = bf16[144,1152]{1,0:T(8,128)(2,1)S(1)} collective-permute-done((bf16[144,1152]{1,0:T(8,128)(2,1)S(1)}, bf16[144,1152]{1,0:T(8,128)(2,1)S(1)}, u32[]{:S(2)}, u32[]{:S(2)}) %collective-permute-start) | collective-permute-done | bytes 331808 | tf_op jit(solution)/shard_map/ppermute | solution.py:35
  16.5 2.8 %collective-permute-start.6 = (bf16[272,1152]{1,0:T(8,128)(2,1)S(1)}, bf16[272,1152]{1,0:T(8,128)(2,1)S(1)}, u32[]{:S(2)}, u32[]{:S(2)}) collective-permute-start(bf16[272,1152]{1,0:T(8,128)(2,1)S(1)} %concatenate.20.near), channel_id=1, source_target_pairs={{0,6},{1,7},{2,0},{3,1},{4,2},{5,3},{6,4},{7,5},{8,56},{9,57},{10,... | collective-permute-start | bytes 1880072 | tf_op jit(solution)/shard_map/ppermute | solution.py:35
  19.4 3.0 %broadcast_select_fusion = (bf16[1152,1152]{1,0:T(8,128)(2,1)S(1)}, bf16[1152,1152]{1,0:T(8,128)(2,1)S(1)}) fusion(bf16[1152,1152]{1,0:T(8,128)(2,1)} %param.10, bf16[1152,1152]{1,0:T(8,128)(2,1)} %param.9, pred[]{:T(512)S(6)} %eq.5), kind=kLoop, calls=%fused_computation | loop fusion | flops 2654208 | bytes 10616833 | tf_op jit(solution)/shard_map/jit(_where)/select_n | solution.py:394
  24.5 4.5 %collective-permute-start.8 = (bf16[800,1152]{1,0:T(8,128)(2,1)S(1)}, bf16[800,1152]{1,0:T(8,128)(2,1)S(1)}, u32[]{:S(2)}, u32[]{:S(2)}) collective-permute-start(bf16[800,1152]{1,0:T(8,128)(2,1)S(1)} %get-tuple-element.17.refs_0_), channel_id=1, source_target_pairs={{0,8},{1,9},{2,10},{3,11},{4,12},{5,13},{6,14},{7,15},{8,0},{9,1},... | collective-permute-start | bytes 5529608 | tf_op jit(solution)/shard_map/ppermute | solution.py:35
  29.0 3.1 %collective-permute-done.6.near = bf16[272,1152]{1,0:T(8,128)(2,1)S(1)} collective-permute-done((bf16[272,1152]{1,0:T(8,128)(2,1)S(1)}, bf16[272,1152]{1,0:T(8,128)(2,1)S(1)}, u32[]{:S(2)}, u32[]{:S(2)}) %collective-permute-start.6) | collective-permute-done | bytes 626720 | tf_op jit(solution)/shard_map/ppermute | solution.py:35
  40.7 2.8 %collective-permute-start.3 = (bf16[272,1152]{1,0:T(8,128)(2,1)S(1)}, bf16[272,1152]{1,0:T(8,128)(2,1)S(1)}, u32[]{:S(2)}, u32[]{:S(2)}) collective-permute-start(bf16[272,1152]{1,0:T(8,128)(2,1)S(1)} %concatenate.22.far), channel_id=1, source_target_pairs={{0,32},{1,33},{2,34},{3,35},{4,36},{5,37},{6,38},{7,39},{8,12},{9,... | collective-permute-start | bytes 1880072 | tf_op jit(solution)/shard_map/ppermute | solution.py:35
  44.8 17.1 %early_pairs.1.early = f32[1536,1152]{1,0:T(8,128)} custom-call(f32[3]{0:T(128)S(1)} %pad_maximum_fusion.3.knob_ref, bf16[800,1152]{1,0:T(8,128)(2,1)S(1)} %get-tuple-element.17.refs_0_, bf16[800,1152]{1,0:T(8,128)(2,1)S(1)} %get-tuple-element.18.refs_1_, bf16[800,1152]{1,0:T(8,128)(2,1)S(1)} %get-tuple-element.19.refs_2_, ...), custom_call_target="tpu_custom_call" | custom-call | flops 10871635968 | bytes 14000000 | tf_op jit(solution)/shard_map/early_pairs/pallas_call | solution.py:196
  65.9 3.5 %collective-permute-done.12.refs_12_ = bf16[272,1152]{1,0:T(8,128)(2,1)} collective-permute-done((bf16[272,1152]{1,0:T(8,128)(2,1)S(1)}, bf16[272,1152]{1,0:T(8,128)(2,1)}, u32[]{:S(2)}, u32[]{:S(2)}) %collective-permute-start.12) | collective-permute-done | bytes 626720 | tf_op jit(solution)/shard_map/ppermute | solution.py:35
  70.4 26.7 %late_pairs.1 = (f32[288,1152]{1,0:T(8,128)}, bf16[288,1152]{1,0:T(8,128)(2,1)}, bf16[288,1152]{1,0:T(8,128)(2,1)}, bf16[288,1152]{1,0:T(8,128)(2,1)}) custom-call(s32[1]{0:T(128)} %bitcast.at_ref, f32[3]{0:T(128)} %copy-done, f32[1536,1152]{1,0:T(8,128)} %early_pairs.1.early, bf16[800,1152]{1,0:T(8,128)(2,1)} %copy-done.1, bf16[800,1152]{1,0:T(8,128)(2,1)} %copy-done.5, ...), custom_call_target="tpu_custom_call" | custom-call | flops 13891534848 | bytes 25000000 | tf_op jit(solution)/shard_map/late_pairs/pallas_call | solution.py:297
  100.7 14.9 %collective-permute-done.13 = bf16[288,1152]{1,0:T(8,128)(2,1)S(1)} collective-permute-done((bf16[288,1152]{1,0:T(8,128)(2,1)}, bf16[288,1152]{1,0:T(8,128)(2,1)S(1)}, u32[]{:S(2)}, u32[]{:S(2)}) %collective-permute-start.13) | collective-permute-done | bytes 663584 | tf_op jit(solution)/shard_map/ppermute | solution.py:35
  117.5 2.5 %collective-permute-start.17 = (f32[72,1152]{1,0:T(8,128)S(1)}, f32[72,1152]{1,0:T(8,128)S(1)}, u32[]{:S(2)}, u32[]{:S(2)}) collective-permute-start(f32[72,1152]{1,0:T(8,128)S(1)} %get-tuple-element.40), channel_id=1, source_target_pairs={{0,48},{1,49},{2,50},{3,51},{4,52},{5,53},{6,54},{7,55},{8,14},{9,... | collective-permute-start | bytes 995336 | tf_op jit(solution)/shard_map/ppermute | solution.py:35
  120.1 8.5 %collective-permute-done.16 = f32[72,1152]{1,0:T(8,128)S(1)} collective-permute-done((f32[72,1152]{1,0:T(8,128)S(1)}, f32[72,1152]{1,0:T(8,128)S(1)}, u32[]{:S(2)}, u32[]{:S(2)}) %collective-permute-start.16) | collective-permute-done | bytes 331808 | tf_op jit(solution)/shard_map/ppermute | solution.py:35
  131.4 2.6 %collective-permute-start.20 = (f32[72,1152]{1,0:T(8,128)S(1)}, f32[72,1152]{1,0:T(8,128)S(1)}, u32[]{:S(2)}, u32[]{:S(2)}) collective-permute-start(f32[72,1152]{1,0:T(8,128)S(1)} %get-tuple-element.35), channel_id=1, source_target_pairs={{0,65},{1,64},{2,67},{3,66},{4,69},{5,68},{6,71},{7,70},{8,73},{9,... | collective-permute-start | bytes 995336 | tf_op jit(solution)/shard_map/ppermute | solution.py:35
  134.6 6.0 %collective-permute-done.19 = f32[72,1152]{1,0:T(8,128)S(1)} collective-permute-done((f32[72,1152]{1,0:T(8,128)S(1)}, f32[72,1152]{1,0:T(8,128)S(1)}, u32[]{:S(2)}, u32[]{:S(2)}) %collective-permute-start.19) | collective-permute-done | bytes 331808 | tf_op jit(solution)/shard_map/ppermute | solution.py:35
  140.7 6.8 %collective-permute-done.21 = f32[72,1152]{1,0:T(8,128)S(1)} collective-permute-done((f32[72,1152]{1,0:T(8,128)S(1)}, f32[72,1152]{1,0:T(8,128)S(1)}, u32[]{:S(2)}, u32[]{:S(2)}) %collective-permute-start.21) | collective-permute-done | bytes 331808 | tf_op jit(solution)/shard_map/ppermute | solution.py:35
  153.5 3.0 %collective-permute-done.24 = bf16[72,1152]{1,0:T(8,128)(2,1)S(1)} collective-permute-done((bf16[72,1152]{1,0:T(8,128)(2,1)S(1)}, bf16[72,1152]{1,0:T(8,128)(2,1)S(1)}, u32[]{:S(2)}, u32[]{:S(2)}) %collective-permute-start.24) | collective-permute-done | bytes 165920 | tf_op jit(solution)/shard_map/ppermute | solution.py:35
  156.6 2.9 %collective-permute-start.26 = (bf16[288,1152]{1,0:T(8,128)(2,1)S(1)}, bf16[288,1152]{1,0:T(8,128)(2,1)S(1)}, u32[]{:S(2)}, u32[]{:S(2)}) collective-permute-start(bf16[288,1152]{1,0:T(8,128)(2,1)S(1)} %constant_dynamic-update-slice_fusion.refs_0_), channel_id=1, source_target_pairs={{0,6},{1,7},{2,0},{3,1},{4,2},{5,3},{6,4},{7,5},{8,56},{9,57},{10,... | collective-permute-start | bytes 1990664 | tf_op jit(solution)/shard_map/ppermute | solution.py:35
  160.6 4.7 %collective-permute-start.28 = (bf16[288,1152]{1,0:T(8,128)(2,1)S(1)}, bf16[288,1152]{1,0:T(8,128)(2,1)S(1)}, u32[]{:S(2)}, u32[]{:S(2)}) collective-permute-start(bf16[288,1152]{1,0:T(8,128)(2,1)S(1)} %constant_dynamic-update-slice_fusion.refs_0_), channel_id=1, source_target_pairs={{0,8},{1,9},{2,10},{3,11},{4,12},{5,13},{6,14},{7,15},{8,0},{9,1},... | collective-permute-start | bytes 1990664 | tf_op jit(solution)/shard_map/ppermute | solution.py:35
  167.8 5.0 %collective-permute-start.29 = (bf16[288,1152]{1,0:T(8,128)(2,1)S(1)}, bf16[288,1152]{1,0:T(8,128)(2,1)S(1)}, u32[]{:S(2)}, u32[]{:S(2)}) collective-permute-start(bf16[288,1152]{1,0:T(8,128)(2,1)S(1)} %collective-permute-done.25.refs_1_), channel_id=1, source_target_pairs={{0,8},{1,9},{2,10},{3,11},{4,12},{5,13},{6,14},{7,15},{8,0},{9,1},... | collective-permute-start | bytes 1990664 | tf_op jit(solution)/shard_map/ppermute | solution.py:35
  174.2 5.3 %collective-permute-start.30 = (bf16[288,1152]{1,0:T(8,128)(2,1)S(1)}, bf16[288,1152]{1,0:T(8,128)(2,1)S(1)}, u32[]{:S(2)}, u32[]{:S(2)}) collective-permute-start(bf16[288,1152]{1,0:T(8,128)(2,1)S(1)} %collective-permute-done.26.refs_2_), channel_id=1, source_target_pairs={{0,8},{1,9},{2,10},{3,11},{4,12},{5,13},{6,14},{7,15},{8,0},{9,1},... | collective-permute-start | bytes 1990664 | tf_op jit(solution)/shard_map/ppermute | solution.py:35
  182.8 4.2 %place.1 = (f32[1152,1152]{1,0:T(8,128)}, f32[1152,1152]{1,0:T(8,128)}) custom-call(bf16[288,1152]{1,0:T(8,128)(2,1)S(1)} %constant_dynamic-update-slice_fusion.refs_0_, bf16[288,1152]{1,0:T(8,128)(2,1)S(1)} %collective-permute-done.25.refs_1_, bf16[288,1152]{1,0:T(8,128)(2,1)S(1)} %collective-permute-done.26.refs_2_, ...), custom_call_target="tpu_custom_call" | custom-call | tf_op jit(solution)/shard_map/place/pallas_call | solution.py:355
  (106 shorter events, 44.3 us)
Async XLA Ops:
  2.7 7.3 %collective-permute-start.2 = (bf16[144,1152]{1,0:T(8,128)(2,1)S(1)}, bf16[144,1152]{1,0:T(8,128)(2,1)S(1)}, u32[]{:S(2)}, u32[]{:S(2)}) collective-permute-start(bf16[144,1152]{1,0:T(8,128)(2,1)S(1)} %get-tuple-element.43), channel_id=1, source_target_pairs={{0,65},{1,64},{2,67},{3,66},{4,69},{5,68},{6,71},{7,70},{8,72},{9,... | collective-permute-start | bytes 995336 | tf_op jit(solution)/shard_map/ppermute | solution.py:35
  5.3 10.7 %collective-permute-start = (bf16[144,1152]{1,0:T(8,128)(2,1)S(1)}, bf16[144,1152]{1,0:T(8,128)(2,1)S(1)}, u32[]{:S(2)}, u32[]{:S(2)}) collective-permute-start(bf16[144,1152]{1,0:T(8,128)(2,1)S(1)} %get-tuple-element.44), channel_id=1, source_target_pairs={{0,64},{1,65},{2,66},{3,67},{4,68},{5,69},{6,70},{7,71},{8,73},{9,... | collective-permute-start | bytes 995336 | tf_op jit(solution)/shard_map/ppermute | solution.py:35
  10.6 18.3 %collective-permute-start.7 = (bf16[272,1152]{1,0:T(8,128)(2,1)S(1)}, bf16[272,1152]{1,0:T(8,128)(2,1)S(1)}, u32[]{:S(2)}, u32[]{:S(2)}) collective-permute-start(bf16[272,1152]{1,0:T(8,128)(2,1)S(1)} %concatenate.22.far), channel_id=1, source_target_pairs={{0,48},{1,49},{2,50},{3,51},{4,52},{5,53},{6,54},{7,55},{8,14},{9,... | collective-permute-start | bytes 1880072 | tf_op jit(solution)/shard_map/ppermute | solution.py:35
  13.2 22.7 %collective-permute-start.5 = (bf16[272,1152]{1,0:T(8,128)(2,1)S(1)}, bf16[272,1152]{1,0:T(8,128)(2,1)S(1)}, u32[]{:S(2)}, u32[]{:S(2)}) collective-permute-start(bf16[272,1152]{1,0:T(8,128)(2,1)S(1)} %concatenate.22.far), channel_id=1, source_target_pairs={{0,16},{1,17},{2,18},{3,19},{4,20},{5,21},{6,22},{7,23},{8,10},{9,... | collective-permute-start | bytes 1880072 | tf_op jit(solution)/shard_map/ppermute | solution.py:35
  16.5 15.5 %collective-permute-start.6 = (bf16[272,1152]{1,0:T(8,128)(2,1)S(1)}, bf16[272,1152]{1,0:T(8,128)(2,1)S(1)}, u32[]{:S(2)}, u32[]{:S(2)}) collective-permute-start(bf16[272,1152]{1,0:T(8,128)(2,1)S(1)} %concatenate.20.near), channel_id=1, source_target_pairs={{0,6},{1,7},{2,0},{3,1},{4,2},{5,3},{6,4},{7,5},{8,56},{9,57},{10,... | collective-permute-start | bytes 1880072 | tf_op jit(solution)/shard_map/ppermute | solution.py:35
  19.4 16.6 %collective-permute-start.4 = (bf16[272,1152]{1,0:T(8,128)(2,1)S(1)}, bf16[272,1152]{1,0:T(8,128)(2,1)S(1)}, u32[]{:S(2)}, u32[]{:S(2)}) collective-permute-start(bf16[272,1152]{1,0:T(8,128)(2,1)S(1)} %concatenate.20.near), channel_id=1, source_target_pairs={{0,2},{1,3},{2,4},{3,5},{4,6},{5,7},{6,0},{7,1},{8,24},{9,25},{10,... | collective-permute-start | bytes 1880072 | tf_op jit(solution)/shard_map/ppermute | solution.py:35
  24.5 20.3 %collective-permute-start.8 = (bf16[800,1152]{1,0:T(8,128)(2,1)S(1)}, bf16[800,1152]{1,0:T(8,128)(2,1)S(1)}, u32[]{:S(2)}, u32[]{:S(2)}) collective-permute-start(bf16[800,1152]{1,0:T(8,128)(2,1)S(1)} %get-tuple-element.17.refs_0_), channel_id=1, source_target_pairs={{0,8},{1,9},{2,10},{3,11},{4,12},{5,13},{6,14},{7,15},{8,0},{9,1},... | collective-permute-start | bytes 5529608 | tf_op jit(solution)/shard_map/ppermute | solution.py:35
  34.2 10.5 %collective-permute-start.10 = (bf16[800,1152]{1,0:T(8,128)(2,1)S(1)}, bf16[800,1152]{1,0:T(8,128)(2,1)S(1)}, u32[]{:S(2)}, u32[]{:S(2)}) collective-permute-start(bf16[800,1152]{1,0:T(8,128)(2,1)S(1)} %get-tuple-element.19.refs_2_), channel_id=1, source_target_pairs={{0,8},{1,9},{2,10},{3,11},{4,12},{5,13},{6,14},{7,15},{8,0},{9,1},... | collective-permute-start | bytes 5529608 | tf_op jit(solution)/shard_map/ppermute | solution.py:35
  40.7 21.3 %collective-permute-start.3 = (bf16[272,1152]{1,0:T(8,128)(2,1)S(1)}, bf16[272,1152]{1,0:T(8,128)(2,1)S(1)}, u32[]{:S(2)}, u32[]{:S(2)}) collective-permute-start(bf16[272,1152]{1,0:T(8,128)(2,1)S(1)} %concatenate.22.far), channel_id=1, source_target_pairs={{0,32},{1,33},{2,34},{3,35},{4,36},{5,37},{6,38},{7,39},{8,12},{9,... | collective-permute-start | bytes 1880072 | tf_op jit(solution)/shard_map/ppermute | solution.py:35
  43.4 18.6 %collective-permute-start.1 = (bf16[272,1152]{1,0:T(8,128)(2,1)S(1)}, bf16[272,1152]{1,0:T(8,128)(2,1)S(1)}, u32[]{:S(2)}, u32[]{:S(2)}) collective-permute-start(bf16[272,1152]{1,0:T(8,128)(2,1)S(1)} %concatenate.20.near), channel_id=1, source_target_pairs={{0,4},{1,5},{2,6},{3,7},{4,0},{5,1},{6,2},{7,3},{8,40},{9,41},{10,... | collective-permute-start | bytes 1880072 | tf_op jit(solution)/shard_map/ppermute | solution.py:35
  97.2 18.4 %collective-permute-start.13 = (bf16[288,1152]{1,0:T(8,128)(2,1)}, bf16[288,1152]{1,0:T(8,128)(2,1)S(1)}, u32[]{:S(2)}, u32[]{:S(2)}) collective-permute-start(bf16[288,1152]{1,0:T(8,128)(2,1)} %get-tuple-element.29), channel_id=1, source_target_pairs={{0,2},{1,3},{2,4},{3,5},{4,6},{5,7},{6,0},{7,1},{8,24},{9,25},{10,... | collective-permute-start | bytes 1990664 | tf_op jit(solution)/shard_map/ppermute | solution.py:35
  98.8 16.8 %collective-permute-start.14 = (bf16[288,1152]{1,0:T(8,128)(2,1)}, bf16[288,1152]{1,0:T(8,128)(2,1)S(1)}, u32[]{:S(2)}, u32[]{:S(2)}) collective-permute-start(bf16[288,1152]{1,0:T(8,128)(2,1)} %get-tuple-element.30), channel_id=1, source_target_pairs={{0,6},{1,7},{2,0},{3,1},{4,2},{5,3},{6,4},{7,5},{8,56},{9,57},{10,... | collective-permute-start | bytes 1990664 | tf_op jit(solution)/shard_map/ppermute | solution.py:35
  99.9 15.7 %collective-permute-start.15 = (bf16[288,1152]{1,0:T(8,128)(2,1)}, bf16[288,1152]{1,0:T(8,128)(2,1)S(1)}, u32[]{:S(2)}, u32[]{:S(2)}) collective-permute-start(bf16[288,1152]{1,0:T(8,128)(2,1)} %get-tuple-element.31), channel_id=1, source_target_pairs={{0,4},{1,5},{2,6},{3,7},{4,0},{5,1},{6,2},{7,3},{8,40},{9,41},{10,... | collective-permute-start | bytes 1990664 | tf_op jit(solution)/shard_map/ppermute | solution.py:35
  117.3 11.2 %collective-permute-start.16 = (f32[72,1152]{1,0:T(8,128)S(1)}, f32[72,1152]{1,0:T(8,128)S(1)}, u32[]{:S(2)}, u32[]{:S(2)}) collective-permute-start(f32[72,1152]{1,0:T(8,128)S(1)} %get-tuple-element.38), channel_id=1, source_target_pairs={{0,16},{1,17},{2,18},{3,19},{4,20},{5,21},{6,22},{7,23},{8,10},{9,... | collective-permute-start | bytes 995336 | tf_op jit(solution)/shard_map/ppermute | solution.py:35
  117.5 11.0 %collective-permute-start.17 = (f32[72,1152]{1,0:T(8,128)S(1)}, f32[72,1152]{1,0:T(8,128)S(1)}, u32[]{:S(2)}, u32[]{:S(2)}) collective-permute-start(f32[72,1152]{1,0:T(8,128)S(1)} %get-tuple-element.40), channel_id=1, source_target_pairs={{0,48},{1,49},{2,50},{3,51},{4,52},{5,53},{6,54},{7,55},{8,14},{9,... | collective-permute-start | bytes 995336 | tf_op jit(solution)/shard_map/ppermute | solution.py:35
  120.1 9.2 %collective-permute-start.18 = (f32[72,1152]{1,0:T(8,128)S(1)}, f32[72,1152]{1,0:T(8,128)}, u32[]{:S(2)}, u32[]{:S(2)}) collective-permute-start(f32[72,1152]{1,0:T(8,128)S(1)} %get-tuple-element.39), channel_id=1, source_target_pairs={{0,32},{1,33},{2,34},{3,35},{4,36},{5,37},{6,38},{7,39},{8,12},{9,... | collective-permute-start | bytes 995336 | tf_op jit(solution)/shard_map/ppermute | solution.py:35
  131.3 9.3 %collective-permute-start.19 = (f32[72,1152]{1,0:T(8,128)S(1)}, f32[72,1152]{1,0:T(8,128)S(1)}, u32[]{:S(2)}, u32[]{:S(2)}) collective-permute-start(f32[72,1152]{1,0:T(8,128)S(1)} %get-tuple-element.35), channel_id=1, source_target_pairs={{0,64},{1,65},{2,66},{3,67},{4,68},{5,69},{6,70},{7,71},{8,72},{9,... | collective-permute-start | bytes 995336 | tf_op jit(solution)/shard_map/ppermute | solution.py:35
  131.4 9.3 %collective-permute-start.20 = (f32[72,1152]{1,0:T(8,128)S(1)}, f32[72,1152]{1,0:T(8,128)S(1)}, u32[]{:S(2)}, u32[]{:S(2)}) collective-permute-start(f32[72,1152]{1,0:T(8,128)S(1)} %get-tuple-element.35), channel_id=1, source_target_pairs={{0,65},{1,64},{2,67},{3,66},{4,69},{5,68},{6,71},{7,70},{8,73},{9,... | collective-permute-start | bytes 995336 | tf_op jit(solution)/shard_map/ppermute | solution.py:35
  134.0 13.5 %collective-permute-start.21 = (f32[72,1152]{1,0:T(8,128)S(1)}, f32[72,1152]{1,0:T(8,128)S(1)}, u32[]{:S(2)}, u32[]{:S(2)}) collective-permute-start(f32[72,1152]{1,0:T(8,128)S(1)} %get-tuple-element.35), channel_id=1, source_target_pairs={{0,1},{1,0},{2,3},{3,2},{4,5},{5,4},{6,7},{7,6},{8,9},{9,8},{10,11... | collective-permute-start | bytes 995336 | tf_op jit(solution)/shard_map/ppermute | solution.py:35
  156.5 11.2 %collective-permute-start.25 = (bf16[288,1152]{1,0:T(8,128)(2,1)S(1)}, bf16[288,1152]{1,0:T(8,128)(2,1)S(1)}, u32[]{:S(2)}, u32[]{:S(2)}) collective-permute-start(bf16[288,1152]{1,0:T(8,128)(2,1)S(1)} %constant_dynamic-update-slice_fusion.refs_0_), channel_id=1, source_target_pairs={{0,2},{1,3},{2,4},{3,5},{4,6},{5,7},{6,0},{7,1},{8,24},{9,25},{10,... | collective-permute-start | bytes 1990664 | tf_op jit(solution)/shard_map/ppermute | solution.py:35
  156.6 17.6 %collective-permute-start.26 = (bf16[288,1152]{1,0:T(8,128)(2,1)S(1)}, bf16[288,1152]{1,0:T(8,128)(2,1)S(1)}, u32[]{:S(2)}, u32[]{:S(2)}) collective-permute-start(bf16[288,1152]{1,0:T(8,128)(2,1)S(1)} %constant_dynamic-update-slice_fusion.refs_0_), channel_id=1, source_target_pairs={{0,6},{1,7},{2,0},{3,1},{4,2},{5,3},{6,4},{7,5},{8,56},{9,57},{10,... | collective-permute-start | bytes 1990664 | tf_op jit(solution)/shard_map/ppermute | solution.py:35
  159.5 20.0 %collective-permute-start.27 = (bf16[288,1152]{1,0:T(8,128)(2,1)S(1)}, bf16[288,1152]{1,0:T(8,128)(2,1)S(1)}, u32[]{:S(2)}, u32[]{:S(2)}) collective-permute-start(bf16[288,1152]{1,0:T(8,128)(2,1)S(1)} %constant_dynamic-update-slice_fusion.refs_0_), channel_id=1, source_target_pairs={{0,4},{1,5},{2,6},{3,7},{4,0},{5,1},{6,2},{7,3},{8,40},{9,41},{10,... | collective-permute-start | bytes 1990664 | tf_op jit(solution)/shard_map/ppermute | solution.py:35
  160.6 20.5 %collective-permute-start.28 = (bf16[288,1152]{1,0:T(8,128)(2,1)S(1)}, bf16[288,1152]{1,0:T(8,128)(2,1)S(1)}, u32[]{:S(2)}, u32[]{:S(2)}) collective-permute-start(bf16[288,1152]{1,0:T(8,128)(2,1)S(1)} %constant_dynamic-update-slice_fusion.refs_0_), channel_id=1, source_target_pairs={{0,8},{1,9},{2,10},{3,11},{4,12},{5,13},{6,14},{7,15},{8,0},{9,1},... | collective-permute-start | bytes 1990664 | tf_op jit(solution)/shard_map/ppermute | solution.py:35
  167.8 13.3 %collective-permute-start.29 = (bf16[288,1152]{1,0:T(8,128)(2,1)S(1)}, bf16[288,1152]{1,0:T(8,128)(2,1)S(1)}, u32[]{:S(2)}, u32[]{:S(2)}) collective-permute-start(bf16[288,1152]{1,0:T(8,128)(2,1)S(1)} %collective-permute-done.25.refs_1_), channel_id=1, source_target_pairs={{0,8},{1,9},{2,10},{3,11},{4,12},{5,13},{6,14},{7,15},{8,0},{9,1},... | collective-permute-start | bytes 1990664 | tf_op jit(solution)/shard_map/ppermute | solution.py:35
  (23 other events, 215.0 us)
